TPU v7x, 32 devices: a whole 2x2x4 slice. The times are simulated.
32 devices in a mesh: shard: 16 (over z, y, core), rep: 2 (over x).
Axes of the slice: x: 2, y: 2, z: 4, core: 2. Of those that a mesh axis runs over, the one named last changes fastest.
Arguments:
- entity: float32 [4096, 256], P(('shard', 'rep')), may hold values from -1.5 to 1.5
- rel_weight: float32 [900, 256], replicated, may hold values from -4 to 4
- tile_rel: int32 [1024], P(('shard', 'rep')), may hold values from 0 to 899
- tile_head: int32 [1024], P(('shard', 'rep')), may hold values from 0 to 1
- tile_tail: int32 [1024], P(('shard', 'rep')), may hold values from 0 to 1
- tile_mask: int32 [1024, 128, 128], P(('shard', 'rep')), may hold values 0 or 1
- negatives: int32 [1024, 256], P(('shard', 'rep')), may hold values from 0 to 255
- tile_count: int32 [32], P(('shard', 'rep')), may hold values from 1 to 32, as said below
Outputs:
- entity_grad: float32 [4096, 256], P(('shard', 'rep'))
- rel_grad: float32 [900, 256], replicated
Inputs may be any that keep to these rules, and one draw needn't show every extreme that they name: `tile_count`: the used slots of a device are its first ones; some device uses all 32.
All inputs are finite; a program needn't handle non-finite values. No bound on the sum of `tile_mask` on one device may be relied on, other than what follows from the above.
Results may differ from a plain program's by a relative error of at most 0.0003.
Values sent between devices are 32-bit elements; how exact they have to be, the bound alone decides.
No kernel may reach another device: no remote copies, remote signals or barrier semaphores. Data moves between devices by JAX's collectives and lax.ppermute only.
A program may use at most 64 MiB of HBM per device.

v0:
```python
import functools

import jax
import jax.numpy as jnp
from jax import lax
from jax.experimental import pallas as pl
from jax.experimental.pallas import tpu as pltpu
from jax.sharding import PartitionSpec as P

AXES = ("shard", "rep")
F32 = jnp.float32
BF16 = jnp.bfloat16
GROUP = 8
LANES = 128
SUBLANES = 8
VMEM_BYTES = 40 * 1024 * 1024
LOG2E = 1.4426950408889634


def halves(value):
    high = value.astype(BF16)
    low = (value - high.astype(F32)).astype(BF16)
    return high, low


def stacked_left(pair, axis):
    return jnp.concatenate([pair[0], pair[0], pair[1]], axis=axis)


def stacked_right(pair, axis):
    return jnp.concatenate([pair[0], pair[1], pair[0]], axis=axis)


def dot(left, right, left_axis, right_axis):
    return lax.dot_general(
        left,
        right,
        dimension_numbers=(((left_axis,), (right_axis,)), ((), ())),
        preferred_element_type=F32,
    )


def prepare_kernel(count, rel_ids, negatives, rel_weight, entity, *refs):
    counts_out, weights_out, names_out, entity_out = refs[:4]
    ids, draws, table, sems = refs[4:]
    tiles, partition = counts_out.shape
    copies = [
        pltpu.make_async_copy(source, target, sems.at[i])
        for i, (source, target) in enumerate(
            [(rel_ids, ids), (negatives, draws), (rel_weight, table), (entity, entity_out)]
        )
    ]
    for copy in copies:
        copy.start()
    copies[1].wait()
    chosen = draws[...]
    columns = lax.broadcasted_iota(jnp.int32, (tiles, partition), 1)
    total = jnp.zeros((tiles, partition), F32)
    for draw in range(chosen.shape[1]):
        total = total + jnp.where(chosen[:, draw : draw + 1] == columns, 1.0, 0.0)
    slots = lax.broadcasted_iota(jnp.int32, (tiles, partition), 0)
    counts_out[...] = jnp.where(slots < count[0], total, 0.0)
    copies[0].wait()
    copies[2].wait()
    lanes = lax.broadcasted_iota(jnp.int32, (1, LANES), 1) % tiles
    names = jnp.zeros((1, LANES), jnp.int32)
    for tile in range(tiles):
        weights_out[tile : tile + 1, :] = table[pl.ds(ids[tile], 1), :]
        names = jnp.where(lanes == tile, ids[tile], names)
    names_out[...] = names.astype(F32)
    copies[3].wait()


def tiles_kernel(blocks, *refs):
    count, place, head_in_ids, tail_in_ids = refs[:4]
    head_in = refs[4 : 4 + blocks]
    tail_in = refs[4 + blocks : 4 + 2 * blocks]
    mask, counts, weights, names = refs[4 + 2 * blocks : 8 + 2 * blocks]
    terms = refs[8 + 2 * blocks]
    head_out, tail_out = refs[9 + 2 * blocks : 11 + 2 * blocks]
    heads, tails, head_grad, tail_grad, head_ids, tail_ids, sems = refs[11 + 2 * blocks :]
    tiles, block, _ = mask.shape
    width = weights.shape[1]
    mine = place[0]
    copies = [
        pltpu.make_async_copy(head_in_ids, head_ids, sems.at[0]),
        pltpu.make_async_copy(tail_in_ids, tail_ids, sems.at[1]),
    ]
    for copy in copies:
        copy.start()
    for k in range(blocks):
        heads[mine ^ k] = head_in[k][...]
        tails[mine ^ k] = tail_in[k][...]
    head_grad[...] = jnp.zeros_like(head_grad)
    terms[2 * tiles :, :] = jnp.zeros((terms.shape[0] - 2 * tiles, LANES), F32)
    terms[2 * tiles : 2 * tiles + 1, :] = names[...]
    tail = tails[...].reshape(blocks * block, width)
    for_scores = stacked_right(halves(tail * -LOG2E), 1)
    for_mixed = stacked_right(halves(tail), 0)
    for copy in copies:
        copy.wait()

    for base in range(0, tiles, GROUP):
        slots = range(base, base + GROUP)
        rows = [heads[head_ids[slot]] for slot in slots]
        scales = [weights[slot : slot + 1, :] for slot in slots]
        scaled = halves(jnp.concatenate([a * b for a, b in zip(rows, scales)], axis=0))
        scores = dot(stacked_left(scaled, 1), for_scores, 1, 1)
        grads = []
        for u, slot in enumerate(slots):
            adjacent = mask[slot]
            live = slot < count[0]
            parts = []
            for b in range(blocks):
                flag = jnp.where(jnp.logical_and(live, tail_ids[slot] == b), 1.0, 0.0)
                times = counts[slot : slot + 1, b * block : (b + 1) * block]
                score = scores[u * block : (u + 1) * block, b * block : (b + 1) * block]
                odds = jnp.exp2(jnp.minimum(score, 115.0))
                parts.append((times - (adjacent * flag) * odds) / (1.0 + odds))
            grads.append(jnp.concatenate(parts, axis=1))
        grads = halves(jnp.concatenate(grads, axis=0))
        mixed = dot(stacked_left(grads, 1), for_mixed, 1, 0)
        for u, slot in enumerate(slots):
            part = mixed[u * block : (u + 1) * block, :]
            term = jnp.sum(rows[u] * part, axis=0, keepdims=True)
            terms[slot : slot + 1, :] = term[:, :LANES]
            terms[tiles + slot : tiles + slot + 1, :] = term[:, LANES:]
            head_grad[head_ids[slot]] += part * scales[u]
        tail_part = dot(stacked_left(grads, 0), stacked_right(scaled, 0), 0, 0).reshape(tail_grad.shape)
        if base == 0:
            tail_grad[...] = tail_part
        else:
            tail_grad[...] += tail_part

    for k in range(blocks):
        head_out[k] = head_grad[mine ^ k]
        tail_out[k] = tail_grad[mine ^ k]


def combine_kernel(gathered, before, out):
    devices = gathered.shape[0]
    tiles = (gathered.shape[1] - SUBLANES) // 2
    rels, width = out.shape
    padded = -(-rels // SUBLANES) * SUBLANES
    share = LANES // tiles
    lanes = lax.broadcasted_iota(jnp.int32, (1, LANES), 1) // tiles
    rows = lax.broadcasted_iota(jnp.int32, (padded, LANES), 0)
    hits = []
    for first in range(0, devices, share):
        names = gathered[first, 2 * tiles : 2 * tiles + 1, :]
        for other in range(1, share):
            names = jnp.where(lanes == other, gathered[first + other, 2 * tiles : 2 * tiles + 1, :], names)
        hits.append(jnp.where(rows == names.astype(jnp.int32), 1.0, 0.0).astype(BF16))
    hits = jnp.concatenate(hits, axis=1)
    left = gathered[:, :tiles, :].reshape(devices * tiles, LANES)
    right = gathered[:, tiles : 2 * tiles, :].reshape(devices * tiles, LANES)
    high, low = halves(jnp.concatenate([left, right], axis=1))
    total = jnp.dot(hits, high, preferred_element_type=F32) + jnp.dot(hits, low, preferred_element_type=F32)

    @pl.when(pl.program_id(0) == 0)
    def _():
        if before is None:
            out[...] = total[:rels]
        else:
            out[...] = before[...] + total[:rels]

    @pl.when(pl.program_id(0) != 0)
    def _():
        out[...] += total[:rels]


def combine(gathered, rels, width, before=None):
    batch = min(gathered.shape[0], 32)
    whole = pl.BlockSpec((rels, width), lambda i: (0, 0))
    kernel = combine_kernel
    operands, in_specs = [gathered], [pl.BlockSpec((batch,) + gathered.shape[1:], lambda i: (i, 0, 0))]
    if before is None:
        kernel = lambda held, out: combine_kernel(held, None, out)
    else:
        operands.append(before)
        in_specs.append(whole)
    return pl.pallas_call(
        kernel,
        out_shape=jax.ShapeDtypeStruct((rels, width), F32),
        grid=(gathered.shape[0] // batch,),
        in_specs=in_specs,
        out_specs=whole,
        compiler_params=pltpu.CompilerParams(vmem_limit_bytes=VMEM_BYTES),
        cost_estimate=pl.CostEstimate(
            flops=4 * rels * gathered.shape[0] * 32 * width, bytes_accessed=2 << 20, transcendentals=0
        ),
        name="combine",
    )(*operands)


def spec(space):
    return pl.BlockSpec(memory_space=space)


def permute(value, shards, reps, shift, flip):
    route = [
        (s * reps + r, (s + shift) % shards * reps + (r ^ flip)) for s in range(shards) for r in range(reps)
    ]
    return lax.ppermute(value, AXES, route)


def exchange(held, bits, index, total):
    ways = 1 << len(bits)
    parts = [held]
    code = sum(((index >> bit) & 1) << i for i, bit in enumerate(bits))
    for k in range(1, ways):
        flip = sum(((k >> i) & 1) << bit for i, bit in enumerate(bits))
        parts.append(lax.ppermute(held, AXES, [(d, d ^ flip) for d in range(total)]))
    for i in range(len(bits)):
        swap = ((code >> i) & 1) == 1
        swapped = [parts[k ^ (1 << i)] for k in range(ways)]
        parts = [jnp.where(swap, b, a) for a, b in zip(parts, swapped)]
    return jnp.concatenate(parts, axis=0)


def local(shards, reps, entity, rel_weight, tile_rel, tile_head, tile_tail, tile_mask, negatives, tile_count):
    tiles = tile_rel.shape[0]
    block, width = entity.shape
    rels = rel_weight.shape[0]
    partition = block * reps
    smem, vmem = spec(pltpu.SMEM), spec(pltpu.VMEM)
    params = pltpu.CompilerParams(vmem_limit_bytes=VMEM_BYTES)

    others = [permute(entity, shards, reps, 0, k) for k in range(1, reps)]
    tails = [permute(entity, shards, reps, 1, k) for k in range(reps)]
    counts, weights, names, own = pl.pallas_call(
        prepare_kernel,
        out_shape=(
            jax.ShapeDtypeStruct((tiles, partition), F32),
            jax.ShapeDtypeStruct((tiles, width), F32),
            jax.ShapeDtypeStruct((1, LANES), F32),
            jax.ShapeDtypeStruct(entity.shape, F32),
        ),
        in_specs=[smem] + [spec(pl.ANY)] * 4,
        out_specs=(vmem, vmem, vmem, vmem),
        scratch_shapes=[
            pltpu.SMEM(tile_rel.shape, jnp.int32),
            pltpu.VMEM(negatives.shape, jnp.int32),
            pltpu.VMEM(rel_weight.shape, F32),
            pltpu.SemaphoreType.DMA((4,)),
        ],
        compiler_params=params,
        cost_estimate=pl.CostEstimate(flops=2 * tiles * partition * 256, bytes_accessed=4 << 20, transcendentals=0),
        name="prepare",
    )(tile_count, tile_rel, negatives, rel_weight, entity)
    mask = tile_mask.astype(F32)
    place = lax.axis_index("rep").astype(jnp.int32)[None]
    pieces = jax.ShapeDtypeStruct((reps, block, width), F32)
    terms, head_parts, tail_parts = pl.pallas_call(
        functools.partial(tiles_kernel, reps),
        out_shape=[jax.ShapeDtypeStruct((2 * tiles + SUBLANES, LANES), F32), pieces, pieces],
        in_specs=[smem] * 2 + [spec(pl.ANY)] * 2 + [vmem] * (2 * reps + 4),
        out_specs=[vmem] * 3,
        scratch_shapes=[pltpu.VMEM((reps, block, width), F32)] * 4
        + [pltpu.SMEM((tiles,), jnp.int32)] * 2
        + [pltpu.SemaphoreType.DMA((2,))],
        compiler_params=params,
        cost_estimate=pl.CostEstimate(
            flops=18 * tiles * block * partition * width, bytes_accessed=4 << 20, transcendentals=0
        ),
        name="tiles",
    )(tile_count, place, tile_head, tile_tail, own, *others, *tails, mask, counts, weights, names)

    total = shards * reps
    low = reps.bit_length() - 1
    top = total.bit_length() - 1
    order = list(range(top - 1, low, -1)) + list(range(low - 1, -1, -1))
    index = lax.axis_index("shard") * reps + lax.axis_index("rep")
    returned = permute(tail_parts, shards, reps, -1, 0)
    held = exchange(terms[None], order[:2], index, total)
    for i in range(2, len(order), 2):
        held = exchange(held, order[i : i + 2], index, total)
    held, returned = lax.optimization_barrier((held, returned))
    theirs = lax.ppermute(held, AXES, [(d, d ^ (1 << low)) for d in range(total)])
    entity_grad = head_parts[0] + returned[0]
    for k in range(1, reps):
        entity_grad = entity_grad + permute(head_parts[k] + returned[k], shards, reps, 0, k)
    half = combine(held, rels, width)
    rel_grad = combine(theirs, rels, width, half)
    return (entity_grad, rel_grad)


def solution(mesh):
    sizes = dict(mesh.shape)
    return jax.shard_map(
        functools.partial(local, sizes["shard"], sizes["rep"]),
        mesh=mesh,
        in_specs=(
            P(AXES, None),
            P(),
            P(AXES),
            P(AXES),
            P(AXES),
            P(AXES, None, None),
            P(AXES, None),
            P(AXES),
        ),
        out_specs=(P(AXES, None), P()),
        check_vma=False,
    )
```

profile of v0, /device:TPU:0, one launch (start us, length us, event | category | flops | bytes accessed | tf_op | source)
XLA Modules:
  0.0 46.1 jit_solution(16473704797520035595)
XLA Ops:
  0.6 3.0 %collective-permute-start = (f32[128,256]{1,0:T(8,128)}, f32[128,256]{1,0:T(8,128)S(1)}, u32[]{:S(2)}, u32[]{:S(2)}) collective-permute-start(f32[128,256]{1,0:T(8,128)} %entity.1), channel_id=1, source_target_pairs={{0,1},{1,0},{2,3},{3,2},{4,5},{5,4},{6,7},{7,6},{8,9},{9,8},{10,11... | collective-permute-start | bytes 393224 | tf_op jit(solution)/shard_map/ppermute | solution.py:204
  3.6 1.8 %collective-permute-start.2 = (f32[128,256]{1,0:T(8,128)}, f32[128,256]{1,0:T(8,128)S(1)}, u32[]{:S(2)}, u32[]{:S(2)}) collective-permute-start(f32[128,256]{1,0:T(8,128)} %entity.1), channel_id=1, source_target_pairs={{0,3},{1,2},{2,5},{3,4},{4,7},{5,6},{6,9},{7,8},{8,11},{9,10},{10,... | collective-permute-start | bytes 393224 | tf_op jit(solution)/shard_map/ppermute | solution.py:204
  6.1 1.8 %convert_element_type.3.refs_8_ = f32[32,128,128]{2,1,0:T(8,128)S(1)} convert(s32[32,128,128]{2,1,0:T(8,128)} %param.13) | non-fusion elementwise | flops 524288 | bytes 4194304 | tf_op jit(solution)/shard_map/convert_element_type | solution.py:251
  8.0 2.2 %prepare.1 = (f32[32,256]{1,0:T(8,128)S(1)}, f32[32,256]{1,0:T(8,128)S(1)}, f32[1,128]{1,0:T(1,128)S(1)}, f32[128,256]{1,0:T(8,128)S(1)}) custom-call(s32[1]{0:T(128)S(6)} %copy.10.count.refs_0_, s32[32]{0:T(128)S(1)} %copy-done.3, s32[32,256]{1,0:T(8,128)S(1)} %copy-done.2, f32[900,256]{1,0:T(8,128)S(1)} %copy-done, f32[128,256]{1,0:T(8,128)S(1)} %copy-done.1), custom_call_target="tpu_custom_call" | custom-call | flops 4194304 | bytes 4194304 | tf_op jit(solution)/shard_map/prepare/pallas_call | solution.py:231
  10.2 1.1 %collective-permute-done.1.refs_6_ = f32[128,256]{1,0:T(8,128)S(1)} collective-permute-done((f32[128,256]{1,0:T(8,128)}, f32[128,256]{1,0:T(8,128)S(1)}, u32[]{:S(2)}, u32[]{:S(2)}) %collective-permute-start.1) | collective-permute-done | bytes 131104 | tf_op jit(solution)/shard_map/ppermute | solution.py:204
  11.4 1.0 %collective-permute-done.2.refs_7_ = f32[128,256]{1,0:T(8,128)S(1)} collective-permute-done((f32[128,256]{1,0:T(8,128)}, f32[128,256]{1,0:T(8,128)S(1)}, u32[]{:S(2)}, u32[]{:S(2)}) %collective-permute-start.2) | collective-permute-done | bytes 131104 | tf_op jit(solution)/shard_map/ppermute | solution.py:204
  12.3 7.5 %tiles.1 = (f32[72,128]{1,0:T(8,128)S(1)}, f32[2,128,256]{2,1,0:T(8,128)S(1)}, f32[2,128,256]{2,1,0:T(8,128)S(1)}) custom-call(s32[1]{0:T(128)S(6)} %copy.10.count.refs_0_, s32[1]{0:T(128)} %bitcast.refs_1_, s32[32]{0:T(128)S(1)} %copy-done.4, s32[32]{0:T(128)S(1)} %copy-done.5, f32[128,256]{1,0:T(8,128)S(1)} %get-tuple-element.11.refs_4_, ...), custom_call_target="tpu_custom_call" | custom-call | flops 4831838208 | bytes 4194304 | tf_op jit(solution)/shard_map/tiles/pallas_call | solution.py:254
  19.9 1.9 %collective-permute-start.3 = (f32[1,72,128]{2,1,0:T(8,128)S(1)}, f32[1,72,128]{2,1,0:T(8,128)S(1)}, u32[]{:S(2)}, u32[]{:S(2)}) collective-permute-start(f32[1,72,128]{2,1,0:T(8,128)S(1)} %bitcast.10), channel_id=1, source_target_pairs={{0,24},{1,25},{2,26},{3,27},{4,28},{5,29},{6,30},{7,31},{8,16},{9,... | collective-permute-start | bytes 110600 | tf_op jit(solution)/shard_map/ppermute | solution.py:213
  21.8 2.5 %collective-permute-start.5 = (f32[1,72,128]{2,1,0:T(8,128)S(1)}, f32[1,72,128]{2,1,0:T(8,128)S(1)}, u32[]{:S(2)}, u32[]{:S(2)}) collective-permute-start(f32[1,72,128]{2,1,0:T(8,128)S(1)} %bitcast.12), channel_id=1, source_target_pairs={{0,16},{1,17},{2,18},{3,19},{4,20},{5,21},{6,22},{7,23},{8,24},{9,... | collective-permute-start | bytes 110600 | tf_op jit(solution)/shard_map/ppermute | solution.py:213
  24.3 1.5 %collective-permute-done.3 = f32[1,72,128]{2,1,0:T(8,128)S(1)} collective-permute-done((f32[1,72,128]{2,1,0:T(8,128)S(1)}, f32[1,72,128]{2,1,0:T(8,128)S(1)}, u32[]{:S(2)}, u32[]{:S(2)}) %collective-permute-start.3) | collective-permute-done | bytes 36896 | tf_op jit(solution)/shard_map/ppermute | solution.py:213
  25.8 0.4 collective-permute-done.4
  26.3 0.8 %collective-permute-done.5 = f32[1,72,128]{2,1,0:T(8,128)S(1)} collective-permute-done((f32[1,72,128]{2,1,0:T(8,128)S(1)}, f32[1,72,128]{2,1,0:T(8,128)S(1)}, u32[]{:S(2)}, u32[]{:S(2)}) %collective-permute-start.5) | collective-permute-done | bytes 36896 | tf_op jit(solution)/shard_map/ppermute | solution.py:213
  27.1 1.3 %collective-permute-start.6 = (f32[4,72,128]{2,1,0:T(8,128)S(1)}, f32[4,72,128]{2,1,0:T(8,128)S(1)}, u32[]{:S(2)}, u32[]{:S(2)}) collective-permute-start(f32[4,72,128]{2,1,0:T(8,128)S(1)} %pad_maximum_fusion.1), channel_id=1, source_target_pairs={{0,5},{1,4},{2,7},{3,6},{4,1},{5,0},{6,3},{7,2},{8,13},{9,12},{10,... | collective-permute-start | bytes 442376 | tf_op jit(solution)/shard_map/ppermute | solution.py:213
  28.4 0.5 %collective-permute-start.7 = (f32[4,72,128]{2,1,0:T(8,128)S(1)}, f32[4,72,128]{2,1,0:T(8,128)S(1)}, u32[]{:S(2)}, u32[]{:S(2)}) collective-permute-start(f32[4,72,128]{2,1,0:T(8,128)S(1)} %pad_maximum_fusion.1), channel_id=1, source_target_pairs={{0,1},{1,0},{2,3},{3,2},{4,5},{5,4},{6,7},{7,6},{8,9},{9,8},{10,11... | collective-permute-start | bytes 442376 | tf_op jit(solution)/shard_map/ppermute | solution.py:213
  29.0 1.7 %collective-permute-start.8 = (f32[4,72,128]{2,1,0:T(8,128)S(1)}, f32[4,72,128]{2,1,0:T(8,128)S(1)}, u32[]{:S(2)}, u32[]{:S(2)}) collective-permute-start(f32[4,72,128]{2,1,0:T(8,128)S(1)} %pad_maximum_fusion.1), channel_id=1, source_target_pairs={{0,4},{1,5},{2,6},{3,7},{4,0},{5,1},{6,2},{7,3},{8,12},{9,13},{10,... | collective-permute-start | bytes 442376 | tf_op jit(solution)/shard_map/ppermute | solution.py:213
  30.6 3.6 %collective-permute-done.6 = f32[4,72,128]{2,1,0:T(8,128)S(1)} collective-permute-done((f32[4,72,128]{2,1,0:T(8,128)S(1)}, f32[4,72,128]{2,1,0:T(8,128)S(1)}, u32[]{:S(2)}, u32[]{:S(2)}) %collective-permute-start.6) | collective-permute-done | bytes 147488 | tf_op jit(solution)/shard_map/ppermute | solution.py:213
  34.2 0.7 %collective-permute-done.7 = f32[4,72,128]{2,1,0:T(8,128)S(1)} collective-permute-done((f32[4,72,128]{2,1,0:T(8,128)S(1)}, f32[4,72,128]{2,1,0:T(8,128)S(1)}, u32[]{:S(2)}, u32[]{:S(2)}) %collective-permute-start.7) | collective-permute-done | bytes 147488 | tf_op jit(solution)/shard_map/ppermute | solution.py:213
  34.9 1.8 %collective-permute-done.8 = f32[4,72,128]{2,1,0:T(8,128)S(1)} collective-permute-done((f32[4,72,128]{2,1,0:T(8,128)S(1)}, f32[4,72,128]{2,1,0:T(8,128)S(1)}, u32[]{:S(2)}, u32[]{:S(2)}) %collective-permute-start.8) | collective-permute-done | bytes 147488 | tf_op jit(solution)/shard_map/ppermute | solution.py:213
  36.9 1.5 %collective-permute-start.11 = (f32[16,72,128]{2,1,0:T(8,128)S(1)}, f32[16,72,128]{2,1,0:T(8,128)S(1)}, u32[]{:S(2)}, u32[]{:S(2)}) collective-permute-start(f32[16,72,128]{2,1,0:T(8,128)S(1)} %pad_maximum_fusion.held), channel_id=1, source_target_pairs={{0,2},{1,3},{2,0},{3,1},{4,6},{5,7},{6,4},{7,5},{8,10},{9,11},{10,... | collective-permute-start | bytes 1769480 | tf_op jit(solution)/shard_map/ppermute | solution.py:279
  38.4 1.2 %collective-permute-start.10 = (f32[128,256]{1,0:T(8,128)S(1)}, f32[128,256]{1,0:T(8,128)S(1)}, u32[]{:S(2)}, u32[]{:S(2)}) collective-permute-start(f32[128,256]{1,0:T(8,128)S(1)} %add_bitcast_fusion), channel_id=1, source_target_pairs={{0,1},{1,0},{2,3},{3,2},{4,5},{5,4},{6,7},{7,6},{8,9},{9,8},{10,11... | collective-permute-start | bytes 393224 | tf_op jit(solution)/shard_map/ppermute | solution.py:204
  39.6 0.6 %combine.2.before = f32[900,256]{1,0:T(8,128)S(1)} custom-call(f32[16,72,128]{2,1,0:T(8,128)S(1)} %pad_maximum_fusion.held), custom_call_target="tpu_custom_call" | custom-call | flops 471859200 | bytes 2097152 | tf_op jit(solution)/shard_map/combine/pallas_call | solution.py:182
  40.2 3.6 %collective-permute-done.10 = f32[128,256]{1,0:T(8,128)S(1)} collective-permute-done((f32[128,256]{1,0:T(8,128)S(1)}, f32[128,256]{1,0:T(8,128)S(1)}, u32[]{:S(2)}, u32[]{:S(2)}) %collective-permute-start.10) | collective-permute-done | bytes 131104 | tf_op jit(solution)/shard_map/ppermute | solution.py:204
  43.8 0.7 %bitcast_add_fusion = f32[128,256]{1,0:T(8,128)} fusion(f32[128,256]{1,0:T(8,128)S(1)} %collective-permute-done.10, f32[2,128,256]{2,1,0:T(8,128)S(1)} %collective-permute-done.9, f32[2,128,256]{2,1,0:T(8,128)S(1)} %get-tuple-element.15), kind=kLoop, calls=%fused_computation.2 | loop fusion | flops 65536 | bytes 524288 | tf_op jit(solution)/shard_map/add | solution.py:282
  44.5 1.6 %combine.3 = f32[900,256]{1,0:T(8,128)} custom-call(f32[16,72,128]{2,1,0:T(8,128)S(1)} %collective-permute-done.11.gathered, f32[900,256]{1,0:T(8,128)S(1)} %combine.2.before), custom_call_target="tpu_custom_call" | custom-call | flops 471859200 | bytes 2097152 | tf_op jit(solution)/shard_map/combine/pallas_call | solution.py:182
  (24 shorter events, 0.2 us)
Async XLA Ops:
  0.6 9.6 %collective-permute-start = (f32[128,256]{1,0:T(8,128)}, f32[128,256]{1,0:T(8,128)S(1)}, u32[]{:S(2)}, u32[]{:S(2)}) collective-permute-start(f32[128,256]{1,0:T(8,128)} %entity.1), channel_id=1, source_target_pairs={{0,1},{1,0},{2,3},{3,2},{4,5},{5,4},{6,7},{7,6},{8,9},{9,8},{10,11... | collective-permute-start | bytes 393224 | tf_op jit(solution)/shard_map/ppermute | solution.py:204
  3.6 7.7 %collective-permute-start.1 = (f32[128,256]{1,0:T(8,128)}, f32[128,256]{1,0:T(8,128)S(1)}, u32[]{:S(2)}, u32[]{:S(2)}) collective-permute-start(f32[128,256]{1,0:T(8,128)} %entity.1), channel_id=1, source_target_pairs={{0,2},{1,3},{2,4},{3,5},{4,6},{5,7},{6,8},{7,9},{8,10},{9,11},{10,... | collective-permute-start | bytes 393224 | tf_op jit(solution)/shard_map/ppermute | solution.py:204
  3.6 8.7 %collective-permute-start.2 = (f32[128,256]{1,0:T(8,128)}, f32[128,256]{1,0:T(8,128)S(1)}, u32[]{:S(2)}, u32[]{:S(2)}) collective-permute-start(f32[128,256]{1,0:T(8,128)} %entity.1), channel_id=1, source_target_pairs={{0,3},{1,2},{2,5},{3,4},{4,7},{5,6},{6,9},{7,8},{8,11},{9,10},{10,... | collective-permute-start | bytes 393224 | tf_op jit(solution)/shard_map/ppermute | solution.py:204
  6.1 1.9 %copy-start = (f32[900,256]{1,0:T(8,128)S(1)}, f32[900,256]{1,0:T(8,128)}, u32[]{:S(2)}) copy-start(f32[900,256]{1,0:T(8,128)} %rel_weight.1) | copy-start | bytes 2764804
  6.1 1.9 %copy-start.1 = (f32[128,256]{1,0:T(8,128)S(1)}, f32[128,256]{1,0:T(8,128)}, u32[]{:S(2)}) copy-start(f32[128,256]{1,0:T(8,128)} %entity.1) | copy-start | bytes 393220
  6.1 1.9 %copy-start.2 = (s32[32,256]{1,0:T(8,128)S(1)}, s32[32,256]{1,0:T(8,128)}, u32[]{:S(2)}) copy-start(s32[32,256]{1,0:T(8,128)} %negatives.1) | copy-start | bytes 98308
  6.1 1.9 %copy-start.3 = (s32[32]{0:T(128)S(1)}, s32[32]{0:T(128)}, u32[]{:S(2)}) copy-start(s32[32]{0:T(128)} %rel_ids.1) | copy-start | bytes 388
  6.1 6.2 %copy-start.4 = (s32[32]{0:T(128)S(1)}, s32[32]{0:T(128)}, u32[]{:S(2)}) copy-start(s32[32]{0:T(128)} %refs_2_.1) | copy-start | bytes 388
  6.1 6.2 %copy-start.5 = (s32[32]{0:T(128)S(1)}, s32[32]{0:T(128)}, u32[]{:S(2)}) copy-start(s32[32]{0:T(128)} %refs_3_.1) | copy-start | bytes 388
  19.9 6.0 %collective-permute-start.3 = (f32[1,72,128]{2,1,0:T(8,128)S(1)}, f32[1,72,128]{2,1,0:T(8,128)S(1)}, u32[]{:S(2)}, u32[]{:S(2)}) collective-permute-start(f32[1,72,128]{2,1,0:T(8,128)S(1)} %bitcast.10), channel_id=1, source_target_pairs={{0,24},{1,25},{2,26},{3,27},{4,28},{5,29},{6,30},{7,31},{8,16},{9,... | collective-permute-start | bytes 110600 | tf_op jit(solution)/shard_map/ppermute | solution.py:213
  21.8 4.5 %collective-permute-start.4 = (f32[1,72,128]{2,1,0:T(8,128)S(1)}, f32[1,72,128]{2,1,0:T(8,128)S(1)}, u32[]{:S(2)}, u32[]{:S(2)}) collective-permute-start(f32[1,72,128]{2,1,0:T(8,128)S(1)} %bitcast.11), channel_id=1, source_target_pairs={{0,8},{1,9},{2,10},{3,11},{4,12},{5,13},{6,14},{7,15},{8,0},{9,1},... | collective-permute-start | bytes 110600 | tf_op jit(solution)/shard_map/ppermute | solution.py:213
  21.8 5.2 %collective-permute-start.5 = (f32[1,72,128]{2,1,0:T(8,128)S(1)}, f32[1,72,128]{2,1,0:T(8,128)S(1)}, u32[]{:S(2)}, u32[]{:S(2)}) collective-permute-start(f32[1,72,128]{2,1,0:T(8,128)S(1)} %bitcast.12), channel_id=1, source_target_pairs={{0,16},{1,17},{2,18},{3,19},{4,20},{5,21},{6,22},{7,23},{8,24},{9,... | collective-permute-start | bytes 110600 | tf_op jit(solution)/shard_map/ppermute | solution.py:213
  27.1 7.2 %collective-permute-start.6 = (f32[4,72,128]{2,1,0:T(8,128)S(1)}, f32[4,72,128]{2,1,0:T(8,128)S(1)}, u32[]{:S(2)}, u32[]{:S(2)}) collective-permute-start(f32[4,72,128]{2,1,0:T(8,128)S(1)} %pad_maximum_fusion.1), channel_id=1, source_target_pairs={{0,5},{1,4},{2,7},{3,6},{4,1},{5,0},{6,3},{7,2},{8,13},{9,12},{10,... | collective-permute-start | bytes 442376 | tf_op jit(solution)/shard_map/ppermute | solution.py:213
  28.4 6.5 %collective-permute-start.7 = (f32[4,72,128]{2,1,0:T(8,128)S(1)}, f32[4,72,128]{2,1,0:T(8,128)S(1)}, u32[]{:S(2)}, u32[]{:S(2)}) collective-permute-start(f32[4,72,128]{2,1,0:T(8,128)S(1)} %pad_maximum_fusion.1), channel_id=1, source_target_pairs={{0,1},{1,0},{2,3},{3,2},{4,5},{5,4},{6,7},{7,6},{8,9},{9,8},{10,11... | collective-permute-start | bytes 442376 | tf_op jit(solution)/shard_map/ppermute | solution.py:213
  29.0 7.7 %collective-permute-start.8 = (f32[4,72,128]{2,1,0:T(8,128)S(1)}, f32[4,72,128]{2,1,0:T(8,128)S(1)}, u32[]{:S(2)}, u32[]{:S(2)}) collective-permute-start(f32[4,72,128]{2,1,0:T(8,128)S(1)} %pad_maximum_fusion.1), channel_id=1, source_target_pairs={{0,4},{1,5},{2,6},{3,7},{4,0},{5,1},{6,2},{7,3},{8,12},{9,13},{10,... | collective-permute-start | bytes 442376 | tf_op jit(solution)/shard_map/ppermute | solution.py:213
  30.6 6.2 %collective-permute-start.9 = (f32[2,128,256]{2,1,0:T(8,128)S(1)}, f32[2,128,256]{2,1,0:T(8,128)S(1)}, u32[]{:S(2)}, u32[]{:S(2)}) collective-permute-start(f32[2,128,256]{2,1,0:T(8,128)S(1)} %get-tuple-element.17), channel_id=1, source_target_pairs={{0,30},{1,31},{2,0},{3,1},{4,2},{5,3},{6,4},{7,5},{8,6},{9,7},{10,... | collective-permute-start | bytes 786440 | tf_op jit(solution)/shard_map/ppermute | solution.py:204
  36.9 7.7 %collective-permute-start.11 = (f32[16,72,128]{2,1,0:T(8,128)S(1)}, f32[16,72,128]{2,1,0:T(8,128)S(1)}, u32[]{:S(2)}, u32[]{:S(2)}) collective-permute-start(f32[16,72,128]{2,1,0:T(8,128)S(1)} %pad_maximum_fusion.held), channel_id=1, source_target_pairs={{0,2},{1,3},{2,0},{3,1},{4,6},{5,7},{6,4},{7,5},{8,10},{9,11},{10,... | collective-permute-start | bytes 1769480 | tf_op jit(solution)/shard_map/ppermute | solution.py:279
  38.4 5.5 %collective-permute-start.10 = (f32[128,256]{1,0:T(8,128)S(1)}, f32[128,256]{1,0:T(8,128)S(1)}, u32[]{:S(2)}, u32[]{:S(2)}) collective-permute-start(f32[128,256]{1,0:T(8,128)S(1)} %add_bitcast_fusion), channel_id=1, source_target_pairs={{0,1},{1,0},{2,3},{3,2},{4,5},{5,4},{6,7},{7,6},{8,9},{9,8},{10,11... | collective-permute-start | bytes 393224 | tf_op jit(solution)/shard_map/ppermute | solution.py:204
where the time goes:
time: 46.3 us; the launch traced here: 46.1 us
  starting transfers between devices  15.5 us (33%)
  waiting for transfers between devices  14.5 us (31%)
  Pallas kernels  12 us (26%)
  other arithmetic  2.68 us (6%)
  between operations  1.44 us (3%)
    ppermute x6, waiting for transfers between devices, exchange(): lax.ppermute(held, AXES, [(d, d ^ flip) for d in range(total)])  8.8 us
    ppermute x6, starting transfers between devices, exchange(): lax.ppermute(held, AXES, [(d, d ^ flip) for d in range(total)])  8.01 us
    pallas_call x1, Pallas kernels, local(): pl.pallas_call(functools.partial(tiles_kernel, reps), out_shape=[jax.Shap...  7.5 us
    ppermute x5, starting transfers between devices, permute(): return lax.ppermute(value, AXES, route)  5.98 us
    ppermute x5, waiting for transfers between devices, permute(): return lax.ppermute(value, AXES, route)  5.73 us
    pallas_call x1, Pallas kernels, local(): pl.pallas_call(prepare_kernel, out_shape=(jax.ShapeDtypeStruct((tiles, pa...  2.24 us
    pallas_call x2, Pallas kernels, combine(): pl.pallas_call(kernel, out_shape=jax.ShapeDtypeStruct((rels, width), F32)...  2.23 us
    convert_element_type x1, other arithmetic, local(): mask = tile_mask.astype(F32)  1.81 us
  transfers between devices with their start and end apart: 12, of which 9 were waited for; matrix products, arithmetic and copies ran while one was open for 6% of the time, Pallas kernels for 6%

commit v1 on v0

--- a/solution.py
+++ b/solution.py
@@ -277,11 +277,12 @@
         held = exchange(held, order[i : i + 2], index, total)
     held, returned = lax.optimization_barrier((held, returned))
     theirs = lax.ppermute(held, AXES, [(d, d ^ (1 << low)) for d in range(total)])
-    entity_grad = head_parts[0] + returned[0]
-    for k in range(1, reps):
-        entity_grad = entity_grad + permute(head_parts[k] + returned[k], shards, reps, 0, k)
+    arrived = [permute(head_parts[k] + returned[k], shards, reps, 0, k) for k in range(1, reps)]
     half = combine(held, rels, width)
     rel_grad = combine(theirs, rels, width, half)
+    entity_grad, _ = lax.optimization_barrier((head_parts[0] + returned[0], rel_grad))
+    for part in arrived:
+        entity_grad = entity_grad + part
     return (entity_grad, rel_grad)
 
 

time: 46.3 us -> 44.7 us (0.965)
  waiting for transfers between devices: 14.5 us -> 12.9 us
    ppermute x5, waiting for transfers between devices: 5.73 us -> 4.13 us  [permute(): return lax.ppermute(value, AXES, route)]
  transfers between devices with their start and end apart: 12 -> 12, of which waited for: 9 -> 9; matrix products, arithmetic and copies ran while one was open for 6% -> 4% of each run, Pallas kernels for 6% -> 10%
where the time goes in v1:
time: 44.7 us; the launch traced here: 44.5 us
  starting transfers between devices  15.5 us (35%)
  waiting for transfers between devices  12.9 us (29%)
  Pallas kernels  12 us (27%)
  other arithmetic  2.68 us (6%)
  between operations  1.45 us (3%)
    ppermute x6, waiting for transfers between devices, exchange(): lax.ppermute(held, AXES, [(d, d ^ flip) for d in range(total)])  8.8 us
    ppermute x6, starting transfers between devices, exchange(): lax.ppermute(held, AXES, [(d, d ^ flip) for d in range(total)])  8.01 us
    pallas_call x1, Pallas kernels, local(): pl.pallas_call(functools.partial(tiles_kernel, reps), out_shape=[jax.Shap...  7.5 us
    ppermute x5, starting transfers between devices, permute(): return lax.ppermute(value, AXES, route)  5.98 us
    ppermute x5, waiting for transfers between devices, permute(): return lax.ppermute(value, AXES, route)  4.13 us
    pallas_call x1, Pallas kernels, local(): pl.pallas_call(prepare_kernel, out_shape=(jax.ShapeDtypeStruct((tiles, pa...  2.24 us
    pallas_call x2, Pallas kernels, combine(): pl.pallas_call(kernel, out_shape=jax.ShapeDtypeStruct((rels, width), F32)...  2.23 us
    convert_element_type x1, other arithmetic, local(): mask = tile_mask.astype(F32)  1.81 us
  transfers between devices with their start and end apart: 12, of which 9 were waited for; matrix products, arithmetic and copies ran while one was open for 4% of the time, Pallas kernels for 10%

profile of v1, /device:TPU:0, one launch (start us, length us, event | category | flops | bytes accessed | tf_op | source)
XLA Modules:
  0.0 44.5 jit_solution(18145254519905621829)
XLA Ops:
  0.6 3.0 %collective-permute-start = (f32[128,256]{1,0:T(8,128)}, f32[128,256]{1,0:T(8,128)S(1)}, u32[]{:S(2)}, u32[]{:S(2)}) collective-permute-start(f32[128,256]{1,0:T(8,128)} %entity.1), channel_id=1, source_target_pairs={{0,1},{1,0},{2,3},{3,2},{4,5},{5,4},{6,7},{7,6},{8,9},{9,8},{10,11... | collective-permute-start | bytes 393224 | tf_op jit(solution)/shard_map/ppermute | solution.py:204
  3.6 1.8 %collective-permute-start.2 = (f32[128,256]{1,0:T(8,128)}, f32[128,256]{1,0:T(8,128)S(1)}, u32[]{:S(2)}, u32[]{:S(2)}) collective-permute-start(f32[128,256]{1,0:T(8,128)} %entity.1), channel_id=1, source_target_pairs={{0,3},{1,2},{2,5},{3,4},{4,7},{5,6},{6,9},{7,8},{8,11},{9,10},{10,... | collective-permute-start | bytes 393224 | tf_op jit(solution)/shard_map/ppermute | solution.py:204
  6.1 1.8 %convert_element_type.3.refs_8_ = f32[32,128,128]{2,1,0:T(8,128)S(1)} convert(s32[32,128,128]{2,1,0:T(8,128)} %param.13) | non-fusion elementwise | flops 524288 | bytes 4194304 | tf_op jit(solution)/shard_map/convert_element_type | solution.py:251
  8.0 2.2 %prepare.1 = (f32[32,256]{1,0:T(8,128)S(1)}, f32[32,256]{1,0:T(8,128)S(1)}, f32[1,128]{1,0:T(1,128)S(1)}, f32[128,256]{1,0:T(8,128)S(1)}) custom-call(s32[1]{0:T(128)S(6)} %copy.10.count.refs_0_, s32[32]{0:T(128)S(1)} %copy-done.3, s32[32,256]{1,0:T(8,128)S(1)} %copy-done.2, f32[900,256]{1,0:T(8,128)S(1)} %copy-done, f32[128,256]{1,0:T(8,128)S(1)} %copy-done.1), custom_call_target="tpu_custom_call" | custom-call | flops 4194304 | bytes 4194304 | tf_op jit(solution)/shard_map/prepare/pallas_call | solution.py:231
  10.2 1.1 %collective-permute-done.1.refs_6_ = f32[128,256]{1,0:T(8,128)S(1)} collective-permute-done((f32[128,256]{1,0:T(8,128)}, f32[128,256]{1,0:T(8,128)S(1)}, u32[]{:S(2)}, u32[]{:S(2)}) %collective-permute-start.1) | collective-permute-done | bytes 131104 | tf_op jit(solution)/shard_map/ppermute | solution.py:204
  11.4 1.0 %collective-permute-done.2.refs_7_ = f32[128,256]{1,0:T(8,128)S(1)} collective-permute-done((f32[128,256]{1,0:T(8,128)}, f32[128,256]{1,0:T(8,128)S(1)}, u32[]{:S(2)}, u32[]{:S(2)}) %collective-permute-start.2) | collective-permute-done | bytes 131104 | tf_op jit(solution)/shard_map/ppermute | solution.py:204
  12.3 7.5 %tiles.1 = (f32[72,128]{1,0:T(8,128)S(1)}, f32[2,128,256]{2,1,0:T(8,128)S(1)}, f32[2,128,256]{2,1,0:T(8,128)S(1)}) custom-call(s32[1]{0:T(128)S(6)} %copy.10.count.refs_0_, s32[1]{0:T(128)} %bitcast.refs_1_, s32[32]{0:T(128)S(1)} %copy-done.4, s32[32]{0:T(128)S(1)} %copy-done.5, f32[128,256]{1,0:T(8,128)S(1)} %get-tuple-element.12.refs_4_, ...), custom_call_target="tpu_custom_call" | custom-call | flops 4831838208 | bytes 4194304 | tf_op jit(solution)/shard_map/tiles/pallas_call | solution.py:254
  19.9 1.9 %collective-permute-start.3 = (f32[1,72,128]{2,1,0:T(8,128)S(1)}, f32[1,72,128]{2,1,0:T(8,128)S(1)}, u32[]{:S(2)}, u32[]{:S(2)}) collective-permute-start(f32[1,72,128]{2,1,0:T(8,128)S(1)} %bitcast.10), channel_id=1, source_target_pairs={{0,24},{1,25},{2,26},{3,27},{4,28},{5,29},{6,30},{7,31},{8,16},{9,... | collective-permute-start | bytes 110600 | tf_op jit(solution)/shard_map/ppermute | solution.py:213
  21.8 2.5 %collective-permute-start.5 = (f32[1,72,128]{2,1,0:T(8,128)S(1)}, f32[1,72,128]{2,1,0:T(8,128)S(1)}, u32[]{:S(2)}, u32[]{:S(2)}) collective-permute-start(f32[1,72,128]{2,1,0:T(8,128)S(1)} %bitcast.12), channel_id=1, source_target_pairs={{0,16},{1,17},{2,18},{3,19},{4,20},{5,21},{6,22},{7,23},{8,24},{9,... | collective-permute-start | bytes 110600 | tf_op jit(solution)/shard_map/ppermute | solution.py:213
  24.3 1.5 %collective-permute-done.3 = f32[1,72,128]{2,1,0:T(8,128)S(1)} collective-permute-done((f32[1,72,128]{2,1,0:T(8,128)S(1)}, f32[1,72,128]{2,1,0:T(8,128)S(1)}, u32[]{:S(2)}, u32[]{:S(2)}) %collective-permute-start.3) | collective-permute-done | bytes 36896 | tf_op jit(solution)/shard_map/ppermute | solution.py:213
  25.8 0.4 collective-permute-done.4
  26.3 0.8 %collective-permute-done.5 = f32[1,72,128]{2,1,0:T(8,128)S(1)} collective-permute-done((f32[1,72,128]{2,1,0:T(8,128)S(1)}, f32[1,72,128]{2,1,0:T(8,128)S(1)}, u32[]{:S(2)}, u32[]{:S(2)}) %collective-permute-start.5) | collective-permute-done | bytes 36896 | tf_op jit(solution)/shard_map/ppermute | solution.py:213
  27.1 1.3 %collective-permute-start.6 = (f32[4,72,128]{2,1,0:T(8,128)S(1)}, f32[4,72,128]{2,1,0:T(8,128)S(1)}, u32[]{:S(2)}, u32[]{:S(2)}) collective-permute-start(f32[4,72,128]{2,1,0:T(8,128)S(1)} %pad_maximum_fusion.1), channel_id=1, source_target_pairs={{0,5},{1,4},{2,7},{3,6},{4,1},{5,0},{6,3},{7,2},{8,13},{9,12},{10,... | collective-permute-start | bytes 442376 | tf_op jit(solution)/shard_map/ppermute | solution.py:213
  28.4 0.5 %collective-permute-start.7 = (f32[4,72,128]{2,1,0:T(8,128)S(1)}, f32[4,72,128]{2,1,0:T(8,128)S(1)}, u32[]{:S(2)}, u32[]{:S(2)}) collective-permute-start(f32[4,72,128]{2,1,0:T(8,128)S(1)} %pad_maximum_fusion.1), channel_id=1, source_target_pairs={{0,1},{1,0},{2,3},{3,2},{4,5},{5,4},{6,7},{7,6},{8,9},{9,8},{10,11... | collective-permute-start | bytes 442376 | tf_op jit(solution)/shard_map/ppermute | solution.py:213
  29.0 1.7 %collective-permute-start.8 = (f32[4,72,128]{2,1,0:T(8,128)S(1)}, f32[4,72,128]{2,1,0:T(8,128)S(1)}, u32[]{:S(2)}, u32[]{:S(2)}) collective-permute-start(f32[4,72,128]{2,1,0:T(8,128)S(1)} %pad_maximum_fusion.1), channel_id=1, source_target_pairs={{0,4},{1,5},{2,6},{3,7},{4,0},{5,1},{6,2},{7,3},{8,12},{9,13},{10,... | collective-permute-start | bytes 442376 | tf_op jit(solution)/shard_map/ppermute | solution.py:213
  30.6 3.6 %collective-permute-done.6 = f32[4,72,128]{2,1,0:T(8,128)S(1)} collective-permute-done((f32[4,72,128]{2,1,0:T(8,128)S(1)}, f32[4,72,128]{2,1,0:T(8,128)S(1)}, u32[]{:S(2)}, u32[]{:S(2)}) %collective-permute-start.6) | collective-permute-done | bytes 147488 | tf_op jit(solution)/shard_map/ppermute | solution.py:213
  34.2 0.7 %collective-permute-done.7 = f32[4,72,128]{2,1,0:T(8,128)S(1)} collective-permute-done((f32[4,72,128]{2,1,0:T(8,128)S(1)}, f32[4,72,128]{2,1,0:T(8,128)S(1)}, u32[]{:S(2)}, u32[]{:S(2)}) %collective-permute-start.7) | collective-permute-done | bytes 147488 | tf_op jit(solution)/shard_map/ppermute | solution.py:213
  34.9 1.8 %collective-permute-done.8 = f32[4,72,128]{2,1,0:T(8,128)S(1)} collective-permute-done((f32[4,72,128]{2,1,0:T(8,128)S(1)}, f32[4,72,128]{2,1,0:T(8,128)S(1)}, u32[]{:S(2)}, u32[]{:S(2)}) %collective-permute-start.8) | collective-permute-done | bytes 147488 | tf_op jit(solution)/shard_map/ppermute | solution.py:213
  36.9 1.5 %collective-permute-start.10 = (f32[16,72,128]{2,1,0:T(8,128)S(1)}, f32[16,72,128]{2,1,0:T(8,128)S(1)}, u32[]{:S(2)}, u32[]{:S(2)}) collective-permute-start(f32[16,72,128]{2,1,0:T(8,128)S(1)} %pad_maximum_fusion.held), channel_id=1, source_target_pairs={{0,2},{1,3},{2,0},{3,1},{4,6},{5,7},{6,4},{7,5},{8,10},{9,11},{10,... | collective-permute-start | bytes 1769480 | tf_op jit(solution)/shard_map/ppermute | solution.py:279
  38.4 1.2 %collective-permute-start.11 = (f32[128,256]{1,0:T(8,128)S(1)}, f32[128,256]{1,0:T(8,128)S(1)}, u32[]{:S(2)}, u32[]{:S(2)}) collective-permute-start(f32[128,256]{1,0:T(8,128)S(1)} %get-tuple-element.25), channel_id=1, source_target_pairs={{0,1},{1,0},{2,3},{3,2},{4,5},{5,4},{6,7},{7,6},{8,9},{9,8},{10,11... | collective-permute-start | bytes 393224 | tf_op jit(solution)/shard_map/ppermute | solution.py:204
  39.6 0.6 %combine.2.before = f32[900,256]{1,0:T(8,128)S(1)} custom-call(f32[16,72,128]{2,1,0:T(8,128)S(1)} %pad_maximum_fusion.held), custom_call_target="tpu_custom_call" | custom-call | flops 471859200 | bytes 2097152 | tf_op jit(solution)/shard_map/combine/pallas_call | solution.py:182
  40.2 1.6 %combine.3 = f32[900,256]{1,0:T(8,128)} custom-call(f32[16,72,128]{2,1,0:T(8,128)S(1)} %collective-permute-done.10.gathered, f32[900,256]{1,0:T(8,128)S(1)} %combine.2.before), custom_call_target="tpu_custom_call" | custom-call | flops 471859200 | bytes 2097152 | tf_op jit(solution)/shard_map/combine/pallas_call | solution.py:182
  41.8 2.0 %collective-permute-done.11 = f32[128,256]{1,0:T(8,128)S(1)} collective-permute-done((f32[128,256]{1,0:T(8,128)S(1)}, f32[128,256]{1,0:T(8,128)S(1)}, u32[]{:S(2)}, u32[]{:S(2)}) %collective-permute-start.11) | collective-permute-done | bytes 131104 | tf_op jit(solution)/shard_map/ppermute | solution.py:204
  43.8 0.7 %add.31 = f32[128,256]{1,0:T(8,128)} add(f32[128,256]{1,0:T(8,128)S(1)} %get-tuple-element.21, f32[128,256]{1,0:T(8,128)S(1)} %collective-permute-done.11) | non-fusion elementwise | flops 32768 | bytes 393216 | tf_op jit(solution)/shard_map/add | solution.py:285
  (24 shorter events, 0.2 us)
Async XLA Ops:
  0.6 9.6 %collective-permute-start = (f32[128,256]{1,0:T(8,128)}, f32[128,256]{1,0:T(8,128)S(1)}, u32[]{:S(2)}, u32[]{:S(2)}) collective-permute-start(f32[128,256]{1,0:T(8,128)} %entity.1), channel_id=1, source_target_pairs={{0,1},{1,0},{2,3},{3,2},{4,5},{5,4},{6,7},{7,6},{8,9},{9,8},{10,11... | collective-permute-start | bytes 393224 | tf_op jit(solution)/shard_map/ppermute | solution.py:204
  3.6 7.7 %collective-permute-start.1 = (f32[128,256]{1,0:T(8,128)}, f32[128,256]{1,0:T(8,128)S(1)}, u32[]{:S(2)}, u32[]{:S(2)}) collective-permute-start(f32[128,256]{1,0:T(8,128)} %entity.1), channel_id=1, source_target_pairs={{0,2},{1,3},{2,4},{3,5},{4,6},{5,7},{6,8},{7,9},{8,10},{9,11},{10,... | collective-permute-start | bytes 393224 | tf_op jit(solution)/shard_map/ppermute | solution.py:204
  3.6 8.7 %collective-permute-start.2 = (f32[128,256]{1,0:T(8,128)}, f32[128,256]{1,0:T(8,128)S(1)}, u32[]{:S(2)}, u32[]{:S(2)}) collective-permute-start(f32[128,256]{1,0:T(8,128)} %entity.1), channel_id=1, source_target_pairs={{0,3},{1,2},{2,5},{3,4},{4,7},{5,6},{6,9},{7,8},{8,11},{9,10},{10,... | collective-permute-start | bytes 393224 | tf_op jit(solution)/shard_map/ppermute | solution.py:204
  6.1 1.9 %copy-start = (f32[900,256]{1,0:T(8,128)S(1)}, f32[900,256]{1,0:T(8,128)}, u32[]{:S(2)}) copy-start(f32[900,256]{1,0:T(8,128)} %rel_weight.1) | copy-start | bytes 2764804
  6.1 1.9 %copy-start.1 = (f32[128,256]{1,0:T(8,128)S(1)}, f32[128,256]{1,0:T(8,128)}, u32[]{:S(2)}) copy-start(f32[128,256]{1,0:T(8,128)} %entity.1) | copy-start | bytes 393220
  6.1 1.9 %copy-start.2 = (s32[32,256]{1,0:T(8,128)S(1)}, s32[32,256]{1,0:T(8,128)}, u32[]{:S(2)}) copy-start(s32[32,256]{1,0:T(8,128)} %negatives.1) | copy-start | bytes 98308
  6.1 1.9 %copy-start.3 = (s32[32]{0:T(128)S(1)}, s32[32]{0:T(128)}, u32[]{:S(2)}) copy-start(s32[32]{0:T(128)} %rel_ids.1) | copy-start | bytes 388
  6.1 6.2 %copy-start.4 = (s32[32]{0:T(128)S(1)}, s32[32]{0:T(128)}, u32[]{:S(2)}) copy-start(s32[32]{0:T(128)} %refs_2_.1) | copy-start | bytes 388
  6.1 6.2 %copy-start.5 = (s32[32]{0:T(128)S(1)}, s32[32]{0:T(128)}, u32[]{:S(2)}) copy-start(s32[32]{0:T(128)} %refs_3_.1) | copy-start | bytes 388
  19.9 6.0 %collective-permute-start.3 = (f32[1,72,128]{2,1,0:T(8,128)S(1)}, f32[1,72,128]{2,1,0:T(8,128)S(1)}, u32[]{:S(2)}, u32[]{:S(2)}) collective-permute-start(f32[1,72,128]{2,1,0:T(8,128)S(1)} %bitcast.10), channel_id=1, source_target_pairs={{0,24},{1,25},{2,26},{3,27},{4,28},{5,29},{6,30},{7,31},{8,16},{9,... | collective-permute-start | bytes 110600 | tf_op jit(solution)/shard_map/ppermute | solution.py:213
  21.8 4.5 %collective-permute-start.4 = (f32[1,72,128]{2,1,0:T(8,128)S(1)}, f32[1,72,128]{2,1,0:T(8,128)S(1)}, u32[]{:S(2)}, u32[]{:S(2)}) collective-permute-start(f32[1,72,128]{2,1,0:T(8,128)S(1)} %bitcast.11), channel_id=1, source_target_pairs={{0,8},{1,9},{2,10},{3,11},{4,12},{5,13},{6,14},{7,15},{8,0},{9,1},... | collective-permute-start | bytes 110600 | tf_op jit(solution)/shard_map/ppermute | solution.py:213
  21.8 5.2 %collective-permute-start.5 = (f32[1,72,128]{2,1,0:T(8,128)S(1)}, f32[1,72,128]{2,1,0:T(8,128)S(1)}, u32[]{:S(2)}, u32[]{:S(2)}) collective-permute-start(f32[1,72,128]{2,1,0:T(8,128)S(1)} %bitcast.12), channel_id=1, source_target_pairs={{0,16},{1,17},{2,18},{3,19},{4,20},{5,21},{6,22},{7,23},{8,24},{9,... | collective-permute-start | bytes 110600 | tf_op jit(solution)/shard_map/ppermute | solution.py:213
  27.1 7.2 %collective-permute-start.6 = (f32[4,72,128]{2,1,0:T(8,128)S(1)}, f32[4,72,128]{2,1,0:T(8,128)S(1)}, u32[]{:S(2)}, u32[]{:S(2)}) collective-permute-start(f32[4,72,128]{2,1,0:T(8,128)S(1)} %pad_maximum_fusion.1), channel_id=1, source_target_pairs={{0,5},{1,4},{2,7},{3,6},{4,1},{5,0},{6,3},{7,2},{8,13},{9,12},{10,... | collective-permute-start | bytes 442376 | tf_op jit(solution)/shard_map/ppermute | solution.py:213
  28.4 6.5 %collective-permute-start.7 = (f32[4,72,128]{2,1,0:T(8,128)S(1)}, f32[4,72,128]{2,1,0:T(8,128)S(1)}, u32[]{:S(2)}, u32[]{:S(2)}) collective-permute-start(f32[4,72,128]{2,1,0:T(8,128)S(1)} %pad_maximum_fusion.1), channel_id=1, source_target_pairs={{0,1},{1,0},{2,3},{3,2},{4,5},{5,4},{6,7},{7,6},{8,9},{9,8},{10,11... | collective-permute-start | bytes 442376 | tf_op jit(solution)/shard_map/ppermute | solution.py:213
  29.0 7.7 %collective-permute-start.8 = (f32[4,72,128]{2,1,0:T(8,128)S(1)}, f32[4,72,128]{2,1,0:T(8,128)S(1)}, u32[]{:S(2)}, u32[]{:S(2)}) collective-permute-start(f32[4,72,128]{2,1,0:T(8,128)S(1)} %pad_maximum_fusion.1), channel_id=1, source_target_pairs={{0,4},{1,5},{2,6},{3,7},{4,0},{5,1},{6,2},{7,3},{8,12},{9,13},{10,... | collective-permute-start | bytes 442376 | tf_op jit(solution)/shard_map/ppermute | solution.py:213
  30.6 6.2 %collective-permute-start.9 = (f32[2,128,256]{2,1,0:T(8,128)S(1)}, f32[2,128,256]{2,1,0:T(8,128)S(1)}, u32[]{:S(2)}, u32[]{:S(2)}) collective-permute-start(f32[2,128,256]{2,1,0:T(8,128)S(1)} %get-tuple-element.18), channel_id=1, source_target_pairs={{0,30},{1,31},{2,0},{3,1},{4,2},{5,3},{6,4},{7,5},{8,6},{9,7},{10,... | collective-permute-start | bytes 786440 | tf_op jit(solution)/shard_map/ppermute | solution.py:204
  36.9 3.4 %collective-permute-start.10 = (f32[16,72,128]{2,1,0:T(8,128)S(1)}, f32[16,72,128]{2,1,0:T(8,128)S(1)}, u32[]{:S(2)}, u32[]{:S(2)}) collective-permute-start(f32[16,72,128]{2,1,0:T(8,128)S(1)} %pad_maximum_fusion.held), channel_id=1, source_target_pairs={{0,2},{1,3},{2,0},{3,1},{4,6},{5,7},{6,4},{7,5},{8,10},{9,11},{10,... | collective-permute-start | bytes 1769480 | tf_op jit(solution)/shard_map/ppermute | solution.py:279
  38.4 5.5 %collective-permute-start.11 = (f32[128,256]{1,0:T(8,128)S(1)}, f32[128,256]{1,0:T(8,128)S(1)}, u32[]{:S(2)}, u32[]{:S(2)}) collective-permute-start(f32[128,256]{1,0:T(8,128)S(1)} %get-tuple-element.25), channel_id=1, source_target_pairs={{0,1},{1,0},{2,3},{3,2},{4,5},{5,4},{6,7},{7,6},{8,9},{9,8},{10,11... | collective-permute-start | bytes 393224 | tf_op jit(solution)/shard_map/ppermute | solution.py:204

commit v2 on v1

--- a/solution.py
+++ b/solution.py
@@ -10,7 +10,8 @@
 AXES = ("shard", "rep")
 F32 = jnp.float32
 BF16 = jnp.bfloat16
-GROUP = 8
+GROUP = 2
+AHEAD = 1
 LANES = 128
 SUBLANES = 8
 VMEM_BYTES = 40 * 1024 * 1024
@@ -100,14 +101,15 @@
     for copy in copies:
         copy.wait()
 
-    for base in range(0, tiles, GROUP):
-        slots = range(base, base + GROUP)
-        rows = [heads[head_ids[slot]] for slot in slots]
-        scales = [weights[slot : slot + 1, :] for slot in slots]
+    def start(base):
+        rows = [heads[head_ids[slot]] for slot in range(base, base + GROUP)]
+        scales = [weights[slot : slot + 1, :] for slot in range(base, base + GROUP)]
         scaled = halves(jnp.concatenate([a * b for a, b in zip(rows, scales)], axis=0))
-        scores = dot(stacked_left(scaled, 1), for_scores, 1, 1)
+        return rows, scales, scaled, dot(stacked_left(scaled, 1), for_scores, 1, 1)
+
+    def weigh(base, scores):
         grads = []
-        for u, slot in enumerate(slots):
+        for u, slot in enumerate(range(base, base + GROUP)):
             adjacent = mask[slot]
             live = slot < count[0]
             parts = []
@@ -118,9 +120,16 @@
                 odds = jnp.exp2(jnp.minimum(score, 115.0))
                 parts.append((times - (adjacent * flag) * odds) / (1.0 + odds))
             grads.append(jnp.concatenate(parts, axis=1))
-        grads = halves(jnp.concatenate(grads, axis=0))
+        return halves(jnp.concatenate(grads, axis=0))
+
+    ahead = [start(base) for base in range(0, AHEAD * GROUP, GROUP)]
+    for base in range(0, tiles, GROUP):
+        if base + AHEAD * GROUP < tiles:
+            ahead.append(start(base + AHEAD * GROUP))
+        rows, scales, scaled, scores = ahead.pop(0)
+        grads = weigh(base, scores)
         mixed = dot(stacked_left(grads, 1), for_mixed, 1, 0)
-        for u, slot in enumerate(slots):
+        for u, slot in enumerate(range(base, base + GROUP)):
             part = mixed[u * block : (u + 1) * block, :]
             term = jnp.sum(rows[u] * part, axis=0, keepdims=True)
             terms[slot : slot + 1, :] = term[:, :LANES]

time: 44.7 us -> 43.2 us (0.966)
  Pallas kernels: 12 us -> 10.5 us
    pallas_call x1, Pallas kernels: 7.5 us -> 6.02 us  [local(): pl.pallas_call(functools.partial(tiles_kernel, reps), out_shape=[jax.Shap...]
  transfers between devices with their start and end apart: 12 -> 12, of which waited for: 9 -> 9; matrix products, arithmetic and copies ran while one was open for 4% -> 5% of each run, Pallas kernels for 10% -> 10%
where the time goes in v2:
time: 43.2 us; the launch traced here: 43 us
  starting transfers between devices  15.5 us (36%)
  waiting for transfers between devices  12.9 us (30%)
  Pallas kernels  10.5 us (24%)
  other arithmetic  2.68 us (6%)
  between operations  1.45 us (3%)
    ppermute x6, waiting for transfers between devices, exchange(): lax.ppermute(held, AXES, [(d, d ^ flip) for d in range(total)])  8.8 us
    ppermute x6, starting transfers between devices, exchange(): lax.ppermute(held, AXES, [(d, d ^ flip) for d in range(total)])  8.01 us
    pallas_call x1, Pallas kernels, local(): pl.pallas_call(functools.partial(tiles_kernel, reps), out_shape=[jax.Shap...  6.02 us
    ppermute x5, starting transfers between devices, permute(): return lax.ppermute(value, AXES, route)  5.98 us
    ppermute x5, waiting for transfers between devices, permute(): return lax.ppermute(value, AXES, route)  4.14 us
    pallas_call x1, Pallas kernels, local(): pl.pallas_call(prepare_kernel, out_shape=(jax.ShapeDtypeStruct((tiles, pa...  2.24 us
    pallas_call x2, Pallas kernels, combine(): pl.pallas_call(kernel, out_shape=jax.ShapeDtypeStruct((rels, width), F32)...  2.23 us
    convert_element_type x1, other arithmetic, local(): mask = tile_mask.astype(F32)  1.81 us
  transfers between devices with their start and end apart: 12, of which 9 were waited for; matrix products, arithmetic and copies ran while one was open for 5% of the time, Pallas kernels for 10%

profile of v2, /device:TPU:0, one launch (start us, length us, event | category | flops | bytes accessed | tf_op | source)
XLA Modules:
  0.0 43.0 jit_solution(10926576514998347029)
XLA Ops:
  0.6 3.0 %collective-permute-start = (f32[128,256]{1,0:T(8,128)}, f32[128,256]{1,0:T(8,128)S(1)}, u32[]{:S(2)}, u32[]{:S(2)}) collective-permute-start(f32[128,256]{1,0:T(8,128)} %entity.1), channel_id=1, source_target_pairs={{0,1},{1,0},{2,3},{3,2},{4,5},{5,4},{6,7},{7,6},{8,9},{9,8},{10,11... | collective-permute-start | bytes 393224 | tf_op jit(solution)/shard_map/ppermute | solution.py:213
  3.6 1.8 %collective-permute-start.2 = (f32[128,256]{1,0:T(8,128)}, f32[128,256]{1,0:T(8,128)S(1)}, u32[]{:S(2)}, u32[]{:S(2)}) collective-permute-start(f32[128,256]{1,0:T(8,128)} %entity.1), channel_id=1, source_target_pairs={{0,3},{1,2},{2,5},{3,4},{4,7},{5,6},{6,9},{7,8},{8,11},{9,10},{10,... | collective-permute-start | bytes 393224 | tf_op jit(solution)/shard_map/ppermute | solution.py:213
  6.1 1.8 %convert_element_type.3.refs_8_ = f32[32,128,128]{2,1,0:T(8,128)S(1)} convert(s32[32,128,128]{2,1,0:T(8,128)} %param.13) | non-fusion elementwise | flops 524288 | bytes 4194304 | tf_op jit(solution)/shard_map/convert_element_type | solution.py:260
  8.0 2.2 %prepare.1 = (f32[32,256]{1,0:T(8,128)S(1)}, f32[32,256]{1,0:T(8,128)S(1)}, f32[1,128]{1,0:T(1,128)S(1)}, f32[128,256]{1,0:T(8,128)S(1)}) custom-call(s32[1]{0:T(128)S(6)} %copy.10.count.refs_0_, s32[32]{0:T(128)S(1)} %copy-done.3, s32[32,256]{1,0:T(8,128)S(1)} %copy-done.2, f32[900,256]{1,0:T(8,128)S(1)} %copy-done, f32[128,256]{1,0:T(8,128)S(1)} %copy-done.1), custom_call_target="tpu_custom_call" | custom-call | flops 4194304 | bytes 4194304 | tf_op jit(solution)/shard_map/prepare/pallas_call | solution.py:240
  10.2 1.1 %collective-permute-done.1.refs_6_ = f32[128,256]{1,0:T(8,128)S(1)} collective-permute-done((f32[128,256]{1,0:T(8,128)}, f32[128,256]{1,0:T(8,128)S(1)}, u32[]{:S(2)}, u32[]{:S(2)}) %collective-permute-start.1) | collective-permute-done | bytes 131104 | tf_op jit(solution)/shard_map/ppermute | solution.py:213
  11.4 1.0 %collective-permute-done.2.refs_7_ = f32[128,256]{1,0:T(8,128)S(1)} collective-permute-done((f32[128,256]{1,0:T(8,128)}, f32[128,256]{1,0:T(8,128)S(1)}, u32[]{:S(2)}, u32[]{:S(2)}) %collective-permute-start.2) | collective-permute-done | bytes 131104 | tf_op jit(solution)/shard_map/ppermute | solution.py:213
  12.3 6.0 %tiles.1 = (f32[72,128]{1,0:T(8,128)S(1)}, f32[2,128,256]{2,1,0:T(8,128)S(1)}, f32[2,128,256]{2,1,0:T(8,128)S(1)}) custom-call(s32[1]{0:T(128)S(6)} %copy.10.count.refs_0_, s32[1]{0:T(128)} %bitcast.refs_1_, s32[32]{0:T(128)S(1)} %copy-done.4, s32[32]{0:T(128)S(1)} %copy-done.5, f32[128,256]{1,0:T(8,128)S(1)} %get-tuple-element.12.refs_4_, ...), custom_call_target="tpu_custom_call" | custom-call | flops 4831838208 | bytes 4194304 | tf_op jit(solution)/shard_map/tiles/pallas_call | solution.py:263
  18.4 1.9 %collective-permute-start.3 = (f32[1,72,128]{2,1,0:T(8,128)S(1)}, f32[1,72,128]{2,1,0:T(8,128)S(1)}, u32[]{:S(2)}, u32[]{:S(2)}) collective-permute-start(f32[1,72,128]{2,1,0:T(8,128)S(1)} %bitcast.10), channel_id=1, source_target_pairs={{0,24},{1,25},{2,26},{3,27},{4,28},{5,29},{6,30},{7,31},{8,16},{9,... | collective-permute-start | bytes 110600 | tf_op jit(solution)/shard_map/ppermute | solution.py:222
  20.3 2.5 %collective-permute-start.5 = (f32[1,72,128]{2,1,0:T(8,128)S(1)}, f32[1,72,128]{2,1,0:T(8,128)S(1)}, u32[]{:S(2)}, u32[]{:S(2)}) collective-permute-start(f32[1,72,128]{2,1,0:T(8,128)S(1)} %bitcast.12), channel_id=1, source_target_pairs={{0,16},{1,17},{2,18},{3,19},{4,20},{5,21},{6,22},{7,23},{8,24},{9,... | collective-permute-start | bytes 110600 | tf_op jit(solution)/shard_map/ppermute | solution.py:222
  22.8 1.5 %collective-permute-done.3 = f32[1,72,128]{2,1,0:T(8,128)S(1)} collective-permute-done((f32[1,72,128]{2,1,0:T(8,128)S(1)}, f32[1,72,128]{2,1,0:T(8,128)S(1)}, u32[]{:S(2)}, u32[]{:S(2)}) %collective-permute-start.3) | collective-permute-done | bytes 36896 | tf_op jit(solution)/shard_map/ppermute | solution.py:222
  24.3 0.4 %collective-permute-done.4 = f32[1,72,128]{2,1,0:T(8,128)S(1)} collective-permute-done((f32[1,72,128]{2,1,0:T(8,128)S(1)}, f32[1,72,128]{2,1,0:T(8,128)S(1)}, u32[]{:S(2)}, u32[]{:S(2)}) %collective-permute-start.4) | collective-permute-done | bytes 36896 | tf_op jit(solution)/shard_map/ppermute | solution.py:222
  24.8 0.8 %collective-permute-done.5 = f32[1,72,128]{2,1,0:T(8,128)S(1)} collective-permute-done((f32[1,72,128]{2,1,0:T(8,128)S(1)}, f32[1,72,128]{2,1,0:T(8,128)S(1)}, u32[]{:S(2)}, u32[]{:S(2)}) %collective-permute-start.5) | collective-permute-done | bytes 36896 | tf_op jit(solution)/shard_map/ppermute | solution.py:222
  25.6 1.4 %collective-permute-start.6 = (f32[4,72,128]{2,1,0:T(8,128)S(1)}, f32[4,72,128]{2,1,0:T(8,128)S(1)}, u32[]{:S(2)}, u32[]{:S(2)}) collective-permute-start(f32[4,72,128]{2,1,0:T(8,128)S(1)} %pad_maximum_fusion.1), channel_id=1, source_target_pairs={{0,5},{1,4},{2,7},{3,6},{4,1},{5,0},{6,3},{7,2},{8,13},{9,12},{10,... | collective-permute-start | bytes 442376 | tf_op jit(solution)/shard_map/ppermute | solution.py:222
  27.0 0.5 %collective-permute-start.7 = (f32[4,72,128]{2,1,0:T(8,128)S(1)}, f32[4,72,128]{2,1,0:T(8,128)S(1)}, u32[]{:S(2)}, u32[]{:S(2)}) collective-permute-start(f32[4,72,128]{2,1,0:T(8,128)S(1)} %pad_maximum_fusion.1), channel_id=1, source_target_pairs={{0,1},{1,0},{2,3},{3,2},{4,5},{5,4},{6,7},{7,6},{8,9},{9,8},{10,11... | collective-permute-start | bytes 442376 | tf_op jit(solution)/shard_map/ppermute | solution.py:222
  27.5 1.7 %collective-permute-start.8 = (f32[4,72,128]{2,1,0:T(8,128)S(1)}, f32[4,72,128]{2,1,0:T(8,128)S(1)}, u32[]{:S(2)}, u32[]{:S(2)}) collective-permute-start(f32[4,72,128]{2,1,0:T(8,128)S(1)} %pad_maximum_fusion.1), channel_id=1, source_target_pairs={{0,4},{1,5},{2,6},{3,7},{4,0},{5,1},{6,2},{7,3},{8,12},{9,13},{10,... | collective-permute-start | bytes 442376 | tf_op jit(solution)/shard_map/ppermute | solution.py:222
  29.2 3.6 %collective-permute-done.6 = f32[4,72,128]{2,1,0:T(8,128)S(1)} collective-permute-done((f32[4,72,128]{2,1,0:T(8,128)S(1)}, f32[4,72,128]{2,1,0:T(8,128)S(1)}, u32[]{:S(2)}, u32[]{:S(2)}) %collective-permute-start.6) | collective-permute-done | bytes 147488 | tf_op jit(solution)/shard_map/ppermute | solution.py:222
  32.8 0.7 %collective-permute-done.7 = f32[4,72,128]{2,1,0:T(8,128)S(1)} collective-permute-done((f32[4,72,128]{2,1,0:T(8,128)S(1)}, f32[4,72,128]{2,1,0:T(8,128)S(1)}, u32[]{:S(2)}, u32[]{:S(2)}) %collective-permute-start.7) | collective-permute-done | bytes 147488 | tf_op jit(solution)/shard_map/ppermute | solution.py:222
  33.4 1.8 %collective-permute-done.8 = f32[4,72,128]{2,1,0:T(8,128)S(1)} collective-permute-done((f32[4,72,128]{2,1,0:T(8,128)S(1)}, f32[4,72,128]{2,1,0:T(8,128)S(1)}, u32[]{:S(2)}, u32[]{:S(2)}) %collective-permute-start.8) | collective-permute-done | bytes 147488 | tf_op jit(solution)/shard_map/ppermute | solution.py:222
  35.4 1.5 %collective-permute-start.10 = (f32[16,72,128]{2,1,0:T(8,128)S(1)}, f32[16,72,128]{2,1,0:T(8,128)S(1)}, u32[]{:S(2)}, u32[]{:S(2)}) collective-permute-start(f32[16,72,128]{2,1,0:T(8,128)S(1)} %pad_maximum_fusion.held), channel_id=1, source_target_pairs={{0,2},{1,3},{2,0},{3,1},{4,6},{5,7},{6,4},{7,5},{8,10},{9,11},{10,... | collective-permute-start | bytes 1769480 | tf_op jit(solution)/shard_map/ppermute | solution.py:288
  36.9 1.2 %collective-permute-start.11 = (f32[128,256]{1,0:T(8,128)S(1)}, f32[128,256]{1,0:T(8,128)S(1)}, u32[]{:S(2)}, u32[]{:S(2)}) collective-permute-start(f32[128,256]{1,0:T(8,128)S(1)} %get-tuple-element.25), channel_id=1, source_target_pairs={{0,1},{1,0},{2,3},{3,2},{4,5},{5,4},{6,7},{7,6},{8,9},{9,8},{10,11... | collective-permute-start | bytes 393224 | tf_op jit(solution)/shard_map/ppermute | solution.py:213
  38.1 0.6 %combine.2.before = f32[900,256]{1,0:T(8,128)S(1)} custom-call(f32[16,72,128]{2,1,0:T(8,128)S(1)} %pad_maximum_fusion.held), custom_call_target="tpu_custom_call" | custom-call | flops 471859200 | bytes 2097152 | tf_op jit(solution)/shard_map/combine/pallas_call | solution.py:191
  38.8 1.6 %combine.3 = f32[900,256]{1,0:T(8,128)} custom-call(f32[16,72,128]{2,1,0:T(8,128)S(1)} %collective-permute-done.10.gathered, f32[900,256]{1,0:T(8,128)S(1)} %combine.2.before), custom_call_target="tpu_custom_call" | custom-call | flops 471859200 | bytes 2097152 | tf_op jit(solution)/shard_map/combine/pallas_call | solution.py:191
  40.3 2.0 %collective-permute-done.11 = f32[128,256]{1,0:T(8,128)S(1)} collective-permute-done((f32[128,256]{1,0:T(8,128)S(1)}, f32[128,256]{1,0:T(8,128)S(1)}, u32[]{:S(2)}, u32[]{:S(2)}) %collective-permute-start.11) | collective-permute-done | bytes 131104 | tf_op jit(solution)/shard_map/ppermute | solution.py:213
  42.4 0.7 %add.31 = f32[128,256]{1,0:T(8,128)} add(f32[128,256]{1,0:T(8,128)S(1)} %get-tuple-element.21, f32[128,256]{1,0:T(8,128)S(1)} %collective-permute-done.11) | non-fusion elementwise | flops 32768 | bytes 393216 | tf_op jit(solution)/shard_map/add | solution.py:294
  (24 shorter events, 0.2 us)
Async XLA Ops:
  0.6 9.6 %collective-permute-start = (f32[128,256]{1,0:T(8,128)}, f32[128,256]{1,0:T(8,128)S(1)}, u32[]{:S(2)}, u32[]{:S(2)}) collective-permute-start(f32[128,256]{1,0:T(8,128)} %entity.1), channel_id=1, source_target_pairs={{0,1},{1,0},{2,3},{3,2},{4,5},{5,4},{6,7},{7,6},{8,9},{9,8},{10,11... | collective-permute-start | bytes 393224 | tf_op jit(solution)/shard_map/ppermute | solution.py:213
  3.6 7.7 %collective-permute-start.1 = (f32[128,256]{1,0:T(8,128)}, f32[128,256]{1,0:T(8,128)S(1)}, u32[]{:S(2)}, u32[]{:S(2)}) collective-permute-start(f32[128,256]{1,0:T(8,128)} %entity.1), channel_id=1, source_target_pairs={{0,2},{1,3},{2,4},{3,5},{4,6},{5,7},{6,8},{7,9},{8,10},{9,11},{10,... | collective-permute-start | bytes 393224 | tf_op jit(solution)/shard_map/ppermute | solution.py:213
  3.6 8.7 %collective-permute-start.2 = (f32[128,256]{1,0:T(8,128)}, f32[128,256]{1,0:T(8,128)S(1)}, u32[]{:S(2)}, u32[]{:S(2)}) collective-permute-start(f32[128,256]{1,0:T(8,128)} %entity.1), channel_id=1, source_target_pairs={{0,3},{1,2},{2,5},{3,4},{4,7},{5,6},{6,9},{7,8},{8,11},{9,10},{10,... | collective-permute-start | bytes 393224 | tf_op jit(solution)/shard_map/ppermute | solution.py:213
  6.1 1.9 %copy-start = (f32[900,256]{1,0:T(8,128)S(1)}, f32[900,256]{1,0:T(8,128)}, u32[]{:S(2)}) copy-start(f32[900,256]{1,0:T(8,128)} %rel_weight.1) | copy-start | bytes 2764804
  6.1 1.9 %copy-start.1 = (f32[128,256]{1,0:T(8,128)S(1)}, f32[128,256]{1,0:T(8,128)}, u32[]{:S(2)}) copy-start(f32[128,256]{1,0:T(8,128)} %entity.1) | copy-start | bytes 393220
  6.1 1.9 %copy-start.2 = (s32[32,256]{1,0:T(8,128)S(1)}, s32[32,256]{1,0:T(8,128)}, u32[]{:S(2)}) copy-start(s32[32,256]{1,0:T(8,128)} %negatives.1) | copy-start | bytes 98308
  6.1 1.9 %copy-start.3 = (s32[32]{0:T(128)S(1)}, s32[32]{0:T(128)}, u32[]{:S(2)}) copy-start(s32[32]{0:T(128)} %rel_ids.1) | copy-start | bytes 388
  6.1 6.2 %copy-start.4 = (s32[32]{0:T(128)S(1)}, s32[32]{0:T(128)}, u32[]{:S(2)}) copy-start(s32[32]{0:T(128)} %refs_2_.1) | copy-start | bytes 388
  6.1 6.2 %copy-start.5 = (s32[32]{0:T(128)S(1)}, s32[32]{0:T(128)}, u32[]{:S(2)}) copy-start(s32[32]{0:T(128)} %refs_3_.1) | copy-start | bytes 388
  18.4 6.0 %collective-permute-start.3 = (f32[1,72,128]{2,1,0:T(8,128)S(1)}, f32[1,72,128]{2,1,0:T(8,128)S(1)}, u32[]{:S(2)}, u32[]{:S(2)}) collective-permute-start(f32[1,72,128]{2,1,0:T(8,128)S(1)} %bitcast.10), channel_id=1, source_target_pairs={{0,24},{1,25},{2,26},{3,27},{4,28},{5,29},{6,30},{7,31},{8,16},{9,... | collective-permute-start | bytes 110600 | tf_op jit(solution)/shard_map/ppermute | solution.py:222
  20.3 4.5 %collective-permute-start.4 = (f32[1,72,128]{2,1,0:T(8,128)S(1)}, f32[1,72,128]{2,1,0:T(8,128)S(1)}, u32[]{:S(2)}, u32[]{:S(2)}) collective-permute-start(f32[1,72,128]{2,1,0:T(8,128)S(1)} %bitcast.11), channel_id=1, source_target_pairs={{0,8},{1,9},{2,10},{3,11},{4,12},{5,13},{6,14},{7,15},{8,0},{9,1},... | collective-permute-start | bytes 110600 | tf_op jit(solution)/shard_map/ppermute | solution.py:222
  20.3 5.2 %collective-permute-start.5 = (f32[1,72,128]{2,1,0:T(8,128)S(1)}, f32[1,72,128]{2,1,0:T(8,128)S(1)}, u32[]{:S(2)}, u32[]{:S(2)}) collective-permute-start(f32[1,72,128]{2,1,0:T(8,128)S(1)} %bitcast.12), channel_id=1, source_target_pairs={{0,16},{1,17},{2,18},{3,19},{4,20},{5,21},{6,22},{7,23},{8,24},{9,... | collective-permute-start | bytes 110600 | tf_op jit(solution)/shard_map/ppermute | solution.py:222
  25.6 7.2 %collective-permute-start.6 = (f32[4,72,128]{2,1,0:T(8,128)S(1)}, f32[4,72,128]{2,1,0:T(8,128)S(1)}, u32[]{:S(2)}, u32[]{:S(2)}) collective-permute-start(f32[4,72,128]{2,1,0:T(8,128)S(1)} %pad_maximum_fusion.1), channel_id=1, source_target_pairs={{0,5},{1,4},{2,7},{3,6},{4,1},{5,0},{6,3},{7,2},{8,13},{9,12},{10,... | collective-permute-start | bytes 442376 | tf_op jit(solution)/shard_map/ppermute | solution.py:222
  27.0 6.5 %collective-permute-start.7 = (f32[4,72,128]{2,1,0:T(8,128)S(1)}, f32[4,72,128]{2,1,0:T(8,128)S(1)}, u32[]{:S(2)}, u32[]{:S(2)}) collective-permute-start(f32[4,72,128]{2,1,0:T(8,128)S(1)} %pad_maximum_fusion.1), channel_id=1, source_target_pairs={{0,1},{1,0},{2,3},{3,2},{4,5},{5,4},{6,7},{7,6},{8,9},{9,8},{10,11... | collective-permute-start | bytes 442376 | tf_op jit(solution)/shard_map/ppermute | solution.py:222
  27.5 7.7 %collective-permute-start.8 = (f32[4,72,128]{2,1,0:T(8,128)S(1)}, f32[4,72,128]{2,1,0:T(8,128)S(1)}, u32[]{:S(2)}, u32[]{:S(2)}) collective-permute-start(f32[4,72,128]{2,1,0:T(8,128)S(1)} %pad_maximum_fusion.1), channel_id=1, source_target_pairs={{0,4},{1,5},{2,6},{3,7},{4,0},{5,1},{6,2},{7,3},{8,12},{9,13},{10,... | collective-permute-start | bytes 442376 | tf_op jit(solution)/shard_map/ppermute | solution.py:222
  29.2 6.2 %collective-permute-start.9 = (f32[2,128,256]{2,1,0:T(8,128)S(1)}, f32[2,128,256]{2,1,0:T(8,128)S(1)}, u32[]{:S(2)}, u32[]{:S(2)}) collective-permute-start(f32[2,128,256]{2,1,0:T(8,128)S(1)} %get-tuple-element.18), channel_id=1, source_target_pairs={{0,30},{1,31},{2,0},{3,1},{4,2},{5,3},{6,4},{7,5},{8,6},{9,7},{10,... | collective-permute-start | bytes 786440 | tf_op jit(solution)/shard_map/ppermute | solution.py:213
  35.4 3.4 %collective-permute-start.10 = (f32[16,72,128]{2,1,0:T(8,128)S(1)}, f32[16,72,128]{2,1,0:T(8,128)S(1)}, u32[]{:S(2)}, u32[]{:S(2)}) collective-permute-start(f32[16,72,128]{2,1,0:T(8,128)S(1)} %pad_maximum_fusion.held), channel_id=1, source_target_pairs={{0,2},{1,3},{2,0},{3,1},{4,6},{5,7},{6,4},{7,5},{8,10},{9,11},{10,... | collective-permute-start | bytes 1769480 | tf_op jit(solution)/shard_map/ppermute | solution.py:288
  36.9 5.5 %collective-permute-start.11 = (f32[128,256]{1,0:T(8,128)S(1)}, f32[128,256]{1,0:T(8,128)S(1)}, u32[]{:S(2)}, u32[]{:S(2)}) collective-permute-start(f32[128,256]{1,0:T(8,128)S(1)} %get-tuple-element.25), channel_id=1, source_target_pairs={{0,1},{1,0},{2,3},{3,2},{4,5},{5,4},{6,7},{7,6},{8,9},{9,8},{10,11... | collective-permute-start | bytes 393224 | tf_op jit(solution)/shard_map/ppermute | solution.py:213

commit v3 on v2

--- a/solution.py
+++ b/solution.py
@@ -14,7 +14,7 @@
 AHEAD = 1
 LANES = 128
 SUBLANES = 8
-VMEM_BYTES = 40 * 1024 * 1024
+MIB = 1024 * 1024
 LOG2E = 1.4426950408889634
 
 
@@ -78,8 +78,8 @@
     tail_in = refs[4 + blocks : 4 + 2 * blocks]
     mask, counts, weights, names = refs[4 + 2 * blocks : 8 + 2 * blocks]
     terms = refs[8 + 2 * blocks]
-    head_out, tail_out = refs[9 + 2 * blocks : 11 + 2 * blocks]
-    heads, tails, head_grad, tail_grad, head_ids, tail_ids, sems = refs[11 + 2 * blocks :]
+    head_out, heads, grads_high, grads_low = refs[9 + 2 * blocks : 13 + 2 * blocks]
+    tails, head_grad, head_ids, tail_ids, sems = refs[13 + 2 * blocks :]
     tiles, block, _ = mask.shape
     width = weights.shape[1]
     mine = place[0]
@@ -135,15 +135,32 @@
             terms[slot : slot + 1, :] = term[:, :LANES]
             terms[tiles + slot : tiles + slot + 1, :] = term[:, LANES:]
             head_grad[head_ids[slot]] += part * scales[u]
-        tail_part = dot(stacked_left(grads, 0), stacked_right(scaled, 0), 0, 0).reshape(tail_grad.shape)
-        if base == 0:
-            tail_grad[...] = tail_part
-        else:
-            tail_grad[...] += tail_part
+        here = slice(base * block, (base + GROUP) * block)
+        grads_high[here, :] = grads[0]
+        grads_low[here, :] = grads[1]
 
     for k in range(blocks):
         head_out[k] = head_grad[mine ^ k]
-        tail_out[k] = tail_grad[mine ^ k]
+
+
+def tails_kernel(place, head_in_ids, heads, weights, grads_high, grads_low, tail_out, tail_grad, head_ids, sem):
+    blocks, block, _ = heads.shape
+    tiles = weights.shape[0]
+    copy = pltpu.make_async_copy(head_in_ids, head_ids, sem)
+    copy.start()
+    copy.wait()
+    for base in range(0, tiles, GROUP):
+        here = slice(base * block, (base + GROUP) * block)
+        scaled = [heads[head_ids[slot]] * weights[slot : slot + 1, :] for slot in range(base, base + GROUP)]
+        scaled = halves(jnp.concatenate(scaled, axis=0))
+        grads = grads_high[here, :], grads_low[here, :]
+        part = dot(stacked_left(grads, 0), stacked_right(scaled, 0), 0, 0).reshape(tail_grad.shape)
+        if base == 0:
+            tail_grad[...] = part
+        else:
+            tail_grad[...] += part
+    for k in range(blocks):
+        tail_out[k] = tail_grad[place[0] ^ k]
 
 
 def combine_kernel(gathered, before, out):
@@ -194,7 +211,7 @@
         grid=(gathered.shape[0] // batch,),
         in_specs=in_specs,
         out_specs=whole,
-        compiler_params=pltpu.CompilerParams(vmem_limit_bytes=VMEM_BYTES),
+        compiler_params=pltpu.CompilerParams(vmem_limit_bytes=24 * MIB),
         cost_estimate=pl.CostEstimate(
             flops=4 * rels * gathered.shape[0] * 32 * width, bytes_accessed=2 << 20, transcendentals=0
         ),
@@ -233,7 +250,7 @@
     rels = rel_weight.shape[0]
     partition = block * reps
     smem, vmem = spec(pltpu.SMEM), spec(pltpu.VMEM)
-    params = pltpu.CompilerParams(vmem_limit_bytes=VMEM_BYTES)
+    params = pltpu.CompilerParams(vmem_limit_bytes=min(8 * reps, 48) * MIB)
 
     others = [permute(entity, shards, reps, 0, k) for k in range(1, reps)]
     tails = [permute(entity, shards, reps, 1, k) for k in range(reps)]
@@ -260,28 +277,47 @@
     mask = tile_mask.astype(F32)
     place = lax.axis_index("rep").astype(jnp.int32)[None]
     pieces = jax.ShapeDtypeStruct((reps, block, width), F32)
-    terms, head_parts, tail_parts = pl.pallas_call(
+    coefficients = jax.ShapeDtypeStruct((tiles * block, partition), BF16)
+    terms, head_parts, heads, grads_high, grads_low = pl.pallas_call(
         functools.partial(tiles_kernel, reps),
-        out_shape=[jax.ShapeDtypeStruct((2 * tiles + SUBLANES, LANES), F32), pieces, pieces],
+        out_shape=[jax.ShapeDtypeStruct((2 * tiles + SUBLANES, LANES), F32), pieces, pieces]
+        + [coefficients] * 2,
         in_specs=[smem] * 2 + [spec(pl.ANY)] * 2 + [vmem] * (2 * reps + 4),
-        out_specs=[vmem] * 3,
-        scratch_shapes=[pltpu.VMEM((reps, block, width), F32)] * 4
+        out_specs=[vmem] * 5,
+        scratch_shapes=[pltpu.VMEM((reps, block, width), F32)] * 2
         + [pltpu.SMEM((tiles,), jnp.int32)] * 2
         + [pltpu.SemaphoreType.DMA((2,))],
         compiler_params=params,
         cost_estimate=pl.CostEstimate(
-            flops=18 * tiles * block * partition * width, bytes_accessed=4 << 20, transcendentals=0
+            flops=12 * tiles * block * partition * width, bytes_accessed=4 << 20, transcendentals=0
         ),
         name="tiles",
     )(tile_count, place, tile_head, tile_tail, own, *others, *tails, mask, counts, weights, names)
+    tail_parts = pl.pallas_call(
+        tails_kernel,
+        out_shape=pieces,
+        in_specs=[smem, spec(pl.ANY)] + [vmem] * 4,
+        out_specs=vmem,
+        scratch_shapes=[
+            pltpu.VMEM((reps, block, width), F32),
+            pltpu.SMEM((tiles,), jnp.int32),
+            pltpu.SemaphoreType.DMA,
+        ],
+        compiler_params=params,
+        cost_estimate=pl.CostEstimate(
+            flops=6 * tiles * block * partition * width, bytes_accessed=4 << 20, transcendentals=0
+        ),
+        name="tails",
+    )(place, tile_head, heads, weights, grads_high, grads_low)
 
     total = shards * reps
     low = reps.bit_length() - 1
     top = total.bit_length() - 1
     order = list(range(top - 1, low, -1)) + list(range(low - 1, -1, -1))
     index = lax.axis_index("shard") * reps + lax.axis_index("rep")
+    held = exchange(terms[None], order[:2], index, total)
+    held, tail_parts = lax.optimization_barrier((held, tail_parts))
     returned = permute(tail_parts, shards, reps, -1, 0)
-    held = exchange(terms[None], order[:2], index, total)
     for i in range(2, len(order), 2):
         held = exchange(held, order[i : i + 2], index, total)
     held, returned = lax.optimization_barrier((held, returned))

time: 43.2 us -> 42.8 us (level)
  waiting for transfers between devices: 12.9 us -> 10.3 us
  Pallas kernels: 10.5 us -> 12.5 us
    ppermute x6, waiting for transfers between devices: 8.8 us -> 6.08 us  [exchange(): lax.ppermute(held, AXES, [(d, d ^ flip) for d in range(total)])]
    pallas_call x0 -> x1, Pallas kernels: none -> 2.53 us  [local(): pl.pallas_call(tails_kernel, out_shape=pieces, in_specs=[smem, spec(pl.AN...]
    pallas_call x1, Pallas kernels: 6.02 us -> 5.52 us  [local(): pl.pallas_call(functools.partial(tiles_kernel, reps), out_shape=[jax.Shap...]
  transfers between devices with their start and end apart: 12 -> 12, of which waited for: 9 -> 7; matrix products, arithmetic and copies ran while one was open for 5% -> 5% of each run, Pallas kernels for 10% -> 16%
where the time goes in v3:
time: 42.8 us; the launch traced here: 42.6 us
  starting transfers between devices  15.7 us (37%)
  Pallas kernels  12.5 us (29%)
  waiting for transfers between devices  10.3 us (24%)
  other arithmetic  2.65 us (6%)
  between operations  1.48 us (3%)
    ppermute x6, starting transfers between devices, exchange(): lax.ppermute(held, AXES, [(d, d ^ flip) for d in range(total)])  8.01 us
    ppermute x5, starting transfers between devices, permute(): return lax.ppermute(value, AXES, route)  6.19 us
    ppermute x6, waiting for transfers between devices, exchange(): lax.ppermute(held, AXES, [(d, d ^ flip) for d in range(total)])  6.08 us
    pallas_call x1, Pallas kernels, local(): pl.pallas_call(functools.partial(tiles_kernel, reps), out_shape=[jax.Shap...  5.52 us
    ppermute x5, waiting for transfers between devices, permute(): return lax.ppermute(value, AXES, route)  4.24 us
    pallas_call x1, Pallas kernels, local(): pl.pallas_call(tails_kernel, out_shape=pieces, in_specs=[smem, spec(pl.AN...  2.53 us
    pallas_call x1, Pallas kernels, local(): pl.pallas_call(prepare_kernel, out_shape=(jax.ShapeDtypeStruct((tiles, pa...  2.24 us
    pallas_call x2, Pallas kernels, combine(): pl.pallas_call(kernel, out_shape=jax.ShapeDtypeStruct((rels, width), F32)...  2.23 us
  transfers between devices with their start and end apart: 12, of which 7 were waited for; matrix products, arithmetic and copies ran while one was open for 5% of the time, Pallas kernels for 16%

profile of v3, /device:TPU:0, one launch (start us, length us, event | category | flops | bytes accessed | tf_op | source)
XLA Modules:
  0.0 42.6 jit_solution(17039442435064098225)
XLA Ops:
  0.6 3.0 %collective-permute-start = (f32[128,256]{1,0:T(8,128)}, f32[128,256]{1,0:T(8,128)S(1)}, u32[]{:S(2)}, u32[]{:S(2)}) collective-permute-start(f32[128,256]{1,0:T(8,128)} %entity.1), channel_id=1, source_target_pairs={{0,1},{1,0},{2,3},{3,2},{4,5},{5,4},{6,7},{7,6},{8,9},{9,8},{10,11... | collective-permute-start | bytes 393224 | tf_op jit(solution)/shard_map/ppermute | solution.py:230
  3.6 1.8 %collective-permute-start.2 = (f32[128,256]{1,0:T(8,128)}, f32[128,256]{1,0:T(8,128)}, u32[]{:S(2)}, u32[]{:S(2)}) collective-permute-start(f32[128,256]{1,0:T(8,128)} %entity.1), channel_id=1, source_target_pairs={{0,3},{1,2},{2,5},{3,4},{4,7},{5,6},{6,9},{7,8},{8,11},{9,10},{10,... | collective-permute-start | bytes 393224 | tf_op jit(solution)/shard_map/ppermute | solution.py:230
  6.1 1.8 %convert_element_type.3.refs_8_ = f32[32,128,128]{2,1,0:T(8,128)S(1)} convert(s32[32,128,128]{2,1,0:T(8,128)} %param.13) | non-fusion elementwise | flops 524288 | bytes 4194304 | tf_op jit(solution)/shard_map/convert_element_type | solution.py:277
  8.0 2.2 %prepare.1 = (f32[32,256]{1,0:T(8,128)S(1)}, f32[32,256]{1,0:T(8,128)S(1)}, f32[1,128]{1,0:T(1,128)S(1)}, f32[128,256]{1,0:T(8,128)S(1)}) custom-call(s32[1]{0:T(128)S(6)} %copy.10.count.refs_0_, s32[32]{0:T(128)S(1)} %copy-done.3, s32[32,256]{1,0:T(8,128)S(1)} %copy-done.2, f32[900,256]{1,0:T(8,128)S(1)} %copy-done, f32[128,256]{1,0:T(8,128)S(1)} %copy-done.1), custom_call_target="tpu_custom_call" | custom-call | flops 4194304 | bytes 4194304 | tf_op jit(solution)/shard_map/prepare/pallas_call | solution.py:257
  10.2 1.1 %collective-permute-done.1.refs_6_ = f32[128,256]{1,0:T(8,128)S(1)} collective-permute-done((f32[128,256]{1,0:T(8,128)}, f32[128,256]{1,0:T(8,128)S(1)}, u32[]{:S(2)}, u32[]{:S(2)}) %collective-permute-start.1) | collective-permute-done | bytes 131104 | tf_op jit(solution)/shard_map/ppermute | solution.py:230
  11.4 1.1 %collective-permute-done.2.refs_7_ = f32[128,256]{1,0:T(8,128)} collective-permute-done((f32[128,256]{1,0:T(8,128)}, f32[128,256]{1,0:T(8,128)}, u32[]{:S(2)}, u32[]{:S(2)}) %collective-permute-start.2) | collective-permute-done | bytes 131104 | tf_op jit(solution)/shard_map/ppermute | solution.py:230
  12.5 5.5 %tiles.1 = (f32[72,128]{1,0:T(8,128)S(1)}, f32[2,128,256]{2,1,0:T(8,128)S(1)}, f32[2,128,256]{2,1,0:T(8,128)S(1)}, bf16[4096,256]{1,0:T(8,128)(2,1)S(1)}, bf16[4096,256]{1,0:T(8,128)(2,1)S(1)}) custom-call(s32[1]{0:T(128)S(6)} %copy.10.count.refs_0_, s32[1]{0:T(128)} %bitcast.refs_1_.place, s32[32]{0:T(128)S(1)} %copy-done.5, s32[32]{0:T(128)S(1)} %copy-done.4, ...), custom_call_target="tpu_custom_call" | custom-call | flops 3221225472 | bytes 4194304 | tf_op jit(solution)/shard_map/tiles/pallas_call | solution.py:281
  18.0 1.9 %collective-permute-start.3 = (f32[1,72,128]{2,1,0:T(8,128)S(1)}, f32[1,72,128]{2,1,0:T(8,128)S(1)}, u32[]{:S(2)}, u32[]{:S(2)}) collective-permute-start(f32[1,72,128]{2,1,0:T(8,128)S(1)} %bitcast.10), channel_id=1, source_target_pairs={{0,24},{1,25},{2,26},{3,27},{4,28},{5,29},{6,30},{7,31},{8,16},{9,... | collective-permute-start | bytes 110600 | tf_op jit(solution)/shard_map/ppermute | solution.py:239
  19.9 2.5 %collective-permute-start.5 = (f32[1,72,128]{2,1,0:T(8,128)S(1)}, f32[1,72,128]{2,1,0:T(8,128)S(1)}, u32[]{:S(2)}, u32[]{:S(2)}) collective-permute-start(f32[1,72,128]{2,1,0:T(8,128)S(1)} %bitcast.12), channel_id=1, source_target_pairs={{0,16},{1,17},{2,18},{3,19},{4,20},{5,21},{6,22},{7,23},{8,24},{9,... | collective-permute-start | bytes 110600 | tf_op jit(solution)/shard_map/ppermute | solution.py:239
  22.4 2.5 %tails.1 = f32[2,128,256]{2,1,0:T(8,128)S(1)} custom-call(s32[1]{0:T(128)} %bitcast.refs_1_.place, s32[32]{0:T(128)S(1)} %copy-done.5, f32[2,128,256]{2,1,0:T(8,128)S(1)} %get-tuple-element.22.heads, f32[32,256]{1,0:T(8,128)S(1)} %get-tuple-element.18.refs_10_.weights, bf16[4096,256]{1,0:T(8,128)(2,1)S(1)} %get-tuple-element.23.grads_high, ...), custom_call_target="tpu_custom_call" | custom-call | flops 1610612736 | bytes 4194304 | tf_op jit(solution)/shard_map/tails/pallas_call | solution.py:296
  25.0 0.2 collective-permute-done.5
  25.2 1.2 %collective-permute-start.6 = (f32[4,72,128]{2,1,0:T(8,128)S(1)}, f32[4,72,128]{2,1,0:T(8,128)S(1)}, u32[]{:S(2)}, u32[]{:S(2)}) collective-permute-start(f32[4,72,128]{2,1,0:T(8,128)S(1)} %pad_maximum_fusion.1), channel_id=1, source_target_pairs={{0,5},{1,4},{2,7},{3,6},{4,1},{5,0},{6,3},{7,2},{8,13},{9,12},{10,... | collective-permute-start | bytes 442376 | tf_op jit(solution)/shard_map/ppermute | solution.py:239
  26.4 0.5 %collective-permute-start.7 = (f32[4,72,128]{2,1,0:T(8,128)S(1)}, f32[4,72,128]{2,1,0:T(8,128)S(1)}, u32[]{:S(2)}, u32[]{:S(2)}) collective-permute-start(f32[4,72,128]{2,1,0:T(8,128)S(1)} %pad_maximum_fusion.1), channel_id=1, source_target_pairs={{0,1},{1,0},{2,3},{3,2},{4,5},{5,4},{6,7},{7,6},{8,9},{9,8},{10,11... | collective-permute-start | bytes 442376 | tf_op jit(solution)/shard_map/ppermute | solution.py:239
  27.0 1.8 %collective-permute-start.8 = (f32[4,72,128]{2,1,0:T(8,128)S(1)}, f32[4,72,128]{2,1,0:T(8,128)S(1)}, u32[]{:S(2)}, u32[]{:S(2)}) collective-permute-start(f32[4,72,128]{2,1,0:T(8,128)S(1)} %pad_maximum_fusion.1), channel_id=1, source_target_pairs={{0,4},{1,5},{2,6},{3,7},{4,0},{5,1},{6,2},{7,3},{8,12},{9,13},{10,... | collective-permute-start | bytes 442376 | tf_op jit(solution)/shard_map/ppermute | solution.py:239
  28.8 0.2 collective-permute-start.9
  29.0 3.4 %collective-permute-done.6 = f32[4,72,128]{2,1,0:T(8,128)S(1)} collective-permute-done((f32[4,72,128]{2,1,0:T(8,128)S(1)}, f32[4,72,128]{2,1,0:T(8,128)S(1)}, u32[]{:S(2)}, u32[]{:S(2)}) %collective-permute-start.6) | collective-permute-done | bytes 147488 | tf_op jit(solution)/shard_map/ppermute | solution.py:239
  32.4 0.7 %collective-permute-done.7 = f32[4,72,128]{2,1,0:T(8,128)S(1)} collective-permute-done((f32[4,72,128]{2,1,0:T(8,128)S(1)}, f32[4,72,128]{2,1,0:T(8,128)S(1)}, u32[]{:S(2)}, u32[]{:S(2)}) %collective-permute-start.7) | collective-permute-done | bytes 147488 | tf_op jit(solution)/shard_map/ppermute | solution.py:239
  33.1 1.8 %collective-permute-done.8 = f32[4,72,128]{2,1,0:T(8,128)S(1)} collective-permute-done((f32[4,72,128]{2,1,0:T(8,128)S(1)}, f32[4,72,128]{2,1,0:T(8,128)S(1)}, u32[]{:S(2)}, u32[]{:S(2)}) %collective-permute-start.8) | collective-permute-done | bytes 147488 | tf_op jit(solution)/shard_map/ppermute | solution.py:239
  35.0 1.5 %collective-permute-start.10 = (f32[16,72,128]{2,1,0:T(8,128)S(1)}, f32[16,72,128]{2,1,0:T(8,128)S(1)}, u32[]{:S(2)}, u32[]{:S(2)}) collective-permute-start(f32[16,72,128]{2,1,0:T(8,128)S(1)} %pad_maximum_fusion.held), channel_id=1, source_target_pairs={{0,2},{1,3},{2,0},{3,1},{4,6},{5,7},{6,4},{7,5},{8,10},{9,11},{10,... | collective-permute-start | bytes 1769480 | tf_op jit(solution)/shard_map/ppermute | solution.py:324
  36.5 1.2 %collective-permute-start.11 = (f32[128,256]{1,0:T(8,128)S(1)}, f32[128,256]{1,0:T(8,128)S(1)}, u32[]{:S(2)}, u32[]{:S(2)}) collective-permute-start(f32[128,256]{1,0:T(8,128)S(1)} %get-tuple-element.34), channel_id=1, source_target_pairs={{0,1},{1,0},{2,3},{3,2},{4,5},{5,4},{6,7},{7,6},{8,9},{9,8},{10,11... | collective-permute-start | bytes 393224 | tf_op jit(solution)/shard_map/ppermute | solution.py:230
  37.7 0.6 %combine.2.before = f32[900,256]{1,0:T(8,128)S(1)} custom-call(f32[16,72,128]{2,1,0:T(8,128)S(1)} %pad_maximum_fusion.held), custom_call_target="tpu_custom_call" | custom-call | flops 471859200 | bytes 2097152 | tf_op jit(solution)/shard_map/combine/pallas_call | solution.py:208
  38.4 1.6 %combine.3 = f32[900,256]{1,0:T(8,128)} custom-call(f32[16,72,128]{2,1,0:T(8,128)S(1)} %collective-permute-done.10.gathered, f32[900,256]{1,0:T(8,128)S(1)} %combine.2.before), custom_call_target="tpu_custom_call" | custom-call | flops 471859200 | bytes 2097152 | tf_op jit(solution)/shard_map/combine/pallas_call | solution.py:208
  39.9 2.0 %collective-permute-done.11 = f32[128,256]{1,0:T(8,128)S(1)} collective-permute-done((f32[128,256]{1,0:T(8,128)S(1)}, f32[128,256]{1,0:T(8,128)S(1)}, u32[]{:S(2)}, u32[]{:S(2)}) %collective-permute-start.11) | collective-permute-done | bytes 131104 | tf_op jit(solution)/shard_map/ppermute | solution.py:230
  42.0 0.7 %add.31 = f32[128,256]{1,0:T(8,128)} add(f32[128,256]{1,0:T(8,128)S(1)} %get-tuple-element.29, f32[128,256]{1,0:T(8,128)S(1)} %collective-permute-done.11) | non-fusion elementwise | flops 32768 | bytes 393216 | tf_op jit(solution)/shard_map/add | solution.py:330
  (24 shorter events, 0.2 us)
Async XLA Ops:
  0.6 9.6 %collective-permute-start = (f32[128,256]{1,0:T(8,128)}, f32[128,256]{1,0:T(8,128)S(1)}, u32[]{:S(2)}, u32[]{:S(2)}) collective-permute-start(f32[128,256]{1,0:T(8,128)} %entity.1), channel_id=1, source_target_pairs={{0,1},{1,0},{2,3},{3,2},{4,5},{5,4},{6,7},{7,6},{8,9},{9,8},{10,11... | collective-permute-start | bytes 393224 | tf_op jit(solution)/shard_map/ppermute | solution.py:230
  3.6 7.7 %collective-permute-start.1 = (f32[128,256]{1,0:T(8,128)}, f32[128,256]{1,0:T(8,128)S(1)}, u32[]{:S(2)}, u32[]{:S(2)}) collective-permute-start(f32[128,256]{1,0:T(8,128)} %entity.1), channel_id=1, source_target_pairs={{0,2},{1,3},{2,4},{3,5},{4,6},{5,7},{6,8},{7,9},{8,10},{9,11},{10,... | collective-permute-start | bytes 393224 | tf_op jit(solution)/shard_map/ppermute | solution.py:230
  3.6 8.8 %collective-permute-start.2 = (f32[128,256]{1,0:T(8,128)}, f32[128,256]{1,0:T(8,128)}, u32[]{:S(2)}, u32[]{:S(2)}) collective-permute-start(f32[128,256]{1,0:T(8,128)} %entity.1), channel_id=1, source_target_pairs={{0,3},{1,2},{2,5},{3,4},{4,7},{5,6},{6,9},{7,8},{8,11},{9,10},{10,... | collective-permute-start | bytes 393224 | tf_op jit(solution)/shard_map/ppermute | solution.py:230
  6.1 1.9 %copy-start = (f32[900,256]{1,0:T(8,128)S(1)}, f32[900,256]{1,0:T(8,128)}, u32[]{:S(2)}) copy-start(f32[900,256]{1,0:T(8,128)} %rel_weight.1) | copy-start | bytes 2764804
  6.1 1.9 %copy-start.1 = (f32[128,256]{1,0:T(8,128)S(1)}, f32[128,256]{1,0:T(8,128)}, u32[]{:S(2)}) copy-start(f32[128,256]{1,0:T(8,128)} %entity.1) | copy-start | bytes 393220
  6.1 1.9 %copy-start.2 = (s32[32,256]{1,0:T(8,128)S(1)}, s32[32,256]{1,0:T(8,128)}, u32[]{:S(2)}) copy-start(s32[32,256]{1,0:T(8,128)} %negatives.1) | copy-start | bytes 98308
  6.1 1.9 %copy-start.3 = (s32[32]{0:T(128)S(1)}, s32[32]{0:T(128)}, u32[]{:S(2)}) copy-start(s32[32]{0:T(128)} %rel_ids.1) | copy-start | bytes 388
  6.1 6.3 %copy-start.4 = (s32[32]{0:T(128)S(1)}, s32[32]{0:T(128)}, u32[]{:S(2)}) copy-start(s32[32]{0:T(128)} %refs_3_.1) | copy-start | bytes 388
  6.1 6.3 %copy-start.5 = (s32[32]{0:T(128)S(1)}, s32[32]{0:T(128)}, u32[]{:S(2)}) copy-start(s32[32]{0:T(128)} %head_in_ids.1) | copy-start | bytes 388
  18.0 7.0 %collective-permute-start.3 = (f32[1,72,128]{2,1,0:T(8,128)S(1)}, f32[1,72,128]{2,1,0:T(8,128)S(1)}, u32[]{:S(2)}, u32[]{:S(2)}) collective-permute-start(f32[1,72,128]{2,1,0:T(8,128)S(1)} %bitcast.10), channel_id=1, source_target_pairs={{0,24},{1,25},{2,26},{3,27},{4,28},{5,29},{6,30},{7,31},{8,16},{9,... | collective-permute-start | bytes 110600 | tf_op jit(solution)/shard_map/ppermute | solution.py:239
  19.9 5.1 %collective-permute-start.4 = (f32[1,72,128]{2,1,0:T(8,128)S(1)}, f32[1,72,128]{2,1,0:T(8,128)S(1)}, u32[]{:S(2)}, u32[]{:S(2)}) collective-permute-start(f32[1,72,128]{2,1,0:T(8,128)S(1)} %bitcast.11), channel_id=1, source_target_pairs={{0,8},{1,9},{2,10},{3,11},{4,12},{5,13},{6,14},{7,15},{8,0},{9,1},... | collective-permute-start | bytes 110600 | tf_op jit(solution)/shard_map/ppermute | solution.py:239
  19.9 5.2 %collective-permute-start.5 = (f32[1,72,128]{2,1,0:T(8,128)S(1)}, f32[1,72,128]{2,1,0:T(8,128)S(1)}, u32[]{:S(2)}, u32[]{:S(2)}) collective-permute-start(f32[1,72,128]{2,1,0:T(8,128)S(1)} %bitcast.12), channel_id=1, source_target_pairs={{0,16},{1,17},{2,18},{3,19},{4,20},{5,21},{6,22},{7,23},{8,24},{9,... | collective-permute-start | bytes 110600 | tf_op jit(solution)/shard_map/ppermute | solution.py:239
  25.2 7.2 %collective-permute-start.6 = (f32[4,72,128]{2,1,0:T(8,128)S(1)}, f32[4,72,128]{2,1,0:T(8,128)S(1)}, u32[]{:S(2)}, u32[]{:S(2)}) collective-permute-start(f32[4,72,128]{2,1,0:T(8,128)S(1)} %pad_maximum_fusion.1), channel_id=1, source_target_pairs={{0,5},{1,4},{2,7},{3,6},{4,1},{5,0},{6,3},{7,2},{8,13},{9,12},{10,... | collective-permute-start | bytes 442376 | tf_op jit(solution)/shard_map/ppermute | solution.py:239
  26.4 6.6 %collective-permute-start.7 = (f32[4,72,128]{2,1,0:T(8,128)S(1)}, f32[4,72,128]{2,1,0:T(8,128)S(1)}, u32[]{:S(2)}, u32[]{:S(2)}) collective-permute-start(f32[4,72,128]{2,1,0:T(8,128)S(1)} %pad_maximum_fusion.1), channel_id=1, source_target_pairs={{0,1},{1,0},{2,3},{3,2},{4,5},{5,4},{6,7},{7,6},{8,9},{9,8},{10,11... | collective-permute-start | bytes 442376 | tf_op jit(solution)/shard_map/ppermute | solution.py:239
  27.0 7.9 %collective-permute-start.8 = (f32[4,72,128]{2,1,0:T(8,128)S(1)}, f32[4,72,128]{2,1,0:T(8,128)S(1)}, u32[]{:S(2)}, u32[]{:S(2)}) collective-permute-start(f32[4,72,128]{2,1,0:T(8,128)S(1)} %pad_maximum_fusion.1), channel_id=1, source_target_pairs={{0,4},{1,5},{2,6},{3,7},{4,0},{5,1},{6,2},{7,3},{8,12},{9,13},{10,... | collective-permute-start | bytes 442376 | tf_op jit(solution)/shard_map/ppermute | solution.py:239
  28.8 6.2 %collective-permute-start.9 = (f32[2,128,256]{2,1,0:T(8,128)S(1)}, f32[2,128,256]{2,1,0:T(8,128)S(1)}, u32[]{:S(2)}, u32[]{:S(2)}) collective-permute-start(f32[2,128,256]{2,1,0:T(8,128)S(1)} %tails.1), channel_id=1, source_target_pairs={{0,30},{1,31},{2,0},{3,1},{4,2},{5,3},{6,4},{7,5},{8,6},{9,7},{10,... | collective-permute-start | bytes 786440 | tf_op jit(solution)/shard_map/ppermute | solution.py:230
  35.0 3.4 %collective-permute-start.10 = (f32[16,72,128]{2,1,0:T(8,128)S(1)}, f32[16,72,128]{2,1,0:T(8,128)S(1)}, u32[]{:S(2)}, u32[]{:S(2)}) collective-permute-start(f32[16,72,128]{2,1,0:T(8,128)S(1)} %pad_maximum_fusion.held), channel_id=1, source_target_pairs={{0,2},{1,3},{2,0},{3,1},{4,6},{5,7},{6,4},{7,5},{8,10},{9,11},{10,... | collective-permute-start | bytes 1769480 | tf_op jit(solution)/shard_map/ppermute | solution.py:324
  36.5 5.5 %collective-permute-start.11 = (f32[128,256]{1,0:T(8,128)S(1)}, f32[128,256]{1,0:T(8,128)S(1)}, u32[]{:S(2)}, u32[]{:S(2)}) collective-permute-start(f32[128,256]{1,0:T(8,128)S(1)} %get-tuple-element.34), channel_id=1, source_target_pairs={{0,1},{1,0},{2,3},{3,2},{4,5},{5,4},{6,7},{7,6},{8,9},{9,8},{10,11... | collective-permute-start | bytes 393224 | tf_op jit(solution)/shard_map/ppermute | solution.py:230

commit v4 on v3

--- a/solution.py
+++ b/solution.py
@@ -74,8 +74,8 @@
 
 def tiles_kernel(blocks, *refs):
     count, place, head_in_ids, tail_in_ids = refs[:4]
-    head_in = refs[4 : 4 + blocks]
-    tail_in = refs[4 + blocks : 4 + 2 * blocks]
+    tail_in = refs[4 : 4 + blocks][::-1]
+    head_in = refs[4 + blocks : 4 + 2 * blocks]
     mask, counts, weights, names = refs[4 + 2 * blocks : 8 + 2 * blocks]
     terms = refs[8 + 2 * blocks]
     head_out, heads, grads_high, grads_low = refs[9 + 2 * blocks : 13 + 2 * blocks]
@@ -252,8 +252,8 @@
     smem, vmem = spec(pltpu.SMEM), spec(pltpu.VMEM)
     params = pltpu.CompilerParams(vmem_limit_bytes=min(8 * reps, 48) * MIB)
 
+    tails = [permute(entity, shards, reps, 1, k) for k in reversed(range(reps))][::-1]
     others = [permute(entity, shards, reps, 0, k) for k in range(1, reps)]
-    tails = [permute(entity, shards, reps, 1, k) for k in range(reps)]
     counts, weights, names, own = pl.pallas_call(
         prepare_kernel,
         out_shape=(
@@ -292,7 +292,7 @@
             flops=12 * tiles * block * partition * width, bytes_accessed=4 << 20, transcendentals=0
         ),
         name="tiles",
-    )(tile_count, place, tile_head, tile_tail, own, *others, *tails, mask, counts, weights, names)
+    )(tile_count, place, tile_head, tile_tail, *tails[::-1], own, *others, mask, counts, weights, names)
     tail_parts = pl.pallas_call(
         tails_kernel,
         out_shape=pieces,

time: 42.8 us -> 42.4 us (level)
    ppermute x5, waiting for transfers between devices: 4.24 us -> 3.28 us  [permute(): return lax.ppermute(value, AXES, route)]
    ppermute x6, waiting for transfers between devices: 6.08 us -> 6.96 us  [exchange(): lax.ppermute(held, AXES, [(d, d ^ flip) for d in range(total)])]
    ppermute x1, starting transfers between devices: 1.47 us -> 0.66 us  [local(): theirs = lax.ppermute(held, AXES, [(d, d ^ 1 << low) for d in range(total)])]
    ppermute x5, starting transfers between devices: 6.19 us -> 6.65 us  [permute(): return lax.ppermute(value, AXES, route)]
  transfers between devices with their start and end apart: 12 -> 12, of which waited for: 7 -> 6; matrix products, arithmetic and copies ran while one was open for 5% -> 5% of each run, Pallas kernels for 16% -> 17%
where the time goes in v4:
time: 42.4 us; the launch traced here: 42.2 us
  starting transfers between devices  15.3 us (36%)
  Pallas kernels  12.5 us (29%)
  waiting for transfers between devices  10.2 us (24%)
  other arithmetic  2.65 us (6%)
  between operations  1.48 us (3%)
    ppermute x6, starting transfers between devices, exchange(): lax.ppermute(held, AXES, [(d, d ^ flip) for d in range(total)])  8.01 us
    ppermute x6, waiting for transfers between devices, exchange(): lax.ppermute(held, AXES, [(d, d ^ flip) for d in range(total)])  6.96 us
    ppermute x5, starting transfers between devices, permute(): return lax.ppermute(value, AXES, route)  6.65 us
    pallas_call x1, Pallas kernels, local(): pl.pallas_call(functools.partial(tiles_kernel, reps), out_shape=[jax.Shap...  5.53 us
    ppermute x5, waiting for transfers between devices, permute(): return lax.ppermute(value, AXES, route)  3.28 us
    pallas_call x1, Pallas kernels, local(): pl.pallas_call(tails_kernel, out_shape=pieces, in_specs=[smem, spec(pl.AN...  2.53 us
    pallas_call x1, Pallas kernels, local(): pl.pallas_call(prepare_kernel, out_shape=(jax.ShapeDtypeStruct((tiles, pa...  2.24 us
    pallas_call x2, Pallas kernels, combine(): pl.pallas_call(kernel, out_shape=jax.ShapeDtypeStruct((rels, width), F32)...  2.23 us
  transfers between devices with their start and end apart: 12, of which 6 were waited for; matrix products, arithmetic and copies ran while one was open for 5% of the time, Pallas kernels for 17%

profile of v4, /device:TPU:0, one launch (start us, length us, event | category | flops | bytes accessed | tf_op | source)
XLA Modules:
  0.0 42.2 jit_solution(5785427569730243823)
XLA Ops:
  0.6 2.4 %collective-permute-start = (f32[128,256]{1,0:T(8,128)}, f32[128,256]{1,0:T(8,128)S(1)}, u32[]{:S(2)}, u32[]{:S(2)}) collective-permute-start(f32[128,256]{1,0:T(8,128)} %entity.1), channel_id=1, source_target_pairs={{0,3},{1,2},{2,5},{3,4},{4,7},{5,6},{6,9},{7,8},{8,11},{9,10},{10,... | collective-permute-start | bytes 393224 | tf_op jit(solution)/shard_map/ppermute | solution.py:230
  3.1 1.6 %collective-permute-start.1 = (f32[128,256]{1,0:T(8,128)}, f32[128,256]{1,0:T(8,128)S(1)}, u32[]{:S(2)}, u32[]{:S(2)}) collective-permute-start(f32[128,256]{1,0:T(8,128)} %entity.1), channel_id=1, source_target_pairs={{0,2},{1,3},{2,4},{3,5},{4,6},{5,7},{6,8},{7,9},{8,10},{9,11},{10,... | collective-permute-start | bytes 393224 | tf_op jit(solution)/shard_map/ppermute | solution.py:230
  4.7 0.5 %collective-permute-start.2 = (f32[128,256]{1,0:T(8,128)}, f32[128,256]{1,0:T(8,128)}, u32[]{:S(2)}, u32[]{:S(2)}) collective-permute-start(f32[128,256]{1,0:T(8,128)} %entity.1), channel_id=1, source_target_pairs={{0,1},{1,0},{2,3},{3,2},{4,5},{5,4},{6,7},{7,6},{8,9},{9,8},{10,11... | collective-permute-start | bytes 393224 | tf_op jit(solution)/shard_map/ppermute | solution.py:230
  5.9 1.8 %convert_element_type.3.refs_8_ = f32[32,128,128]{2,1,0:T(8,128)S(1)} convert(s32[32,128,128]{2,1,0:T(8,128)} %param.13) | non-fusion elementwise | flops 524288 | bytes 4194304 | tf_op jit(solution)/shard_map/convert_element_type | solution.py:277
  7.8 2.2 %prepare.1 = (f32[32,256]{1,0:T(8,128)S(1)}, f32[32,256]{1,0:T(8,128)S(1)}, f32[1,128]{1,0:T(1,128)S(1)}, f32[128,256]{1,0:T(8,128)S(1)}) custom-call(s32[1]{0:T(128)S(6)} %copy.10.count.refs_0_, s32[32]{0:T(128)S(1)} %copy-done.3, s32[32,256]{1,0:T(8,128)S(1)} %copy-done.2, f32[900,256]{1,0:T(8,128)S(1)} %copy-done, f32[128,256]{1,0:T(8,128)S(1)} %copy-done.1), custom_call_target="tpu_custom_call" | custom-call | flops 4194304 | bytes 4194304 | tf_op jit(solution)/shard_map/prepare/pallas_call | solution.py:257
  10.1 1.8 %collective-permute-done.1.refs_5_ = f32[128,256]{1,0:T(8,128)S(1)} collective-permute-done((f32[128,256]{1,0:T(8,128)}, f32[128,256]{1,0:T(8,128)S(1)}, u32[]{:S(2)}, u32[]{:S(2)}) %collective-permute-start.1) | collective-permute-done | bytes 131104 | tf_op jit(solution)/shard_map/ppermute | solution.py:230
  11.8 5.5 %tiles.1 = (f32[72,128]{1,0:T(8,128)S(1)}, f32[2,128,256]{2,1,0:T(8,128)S(1)}, f32[2,128,256]{2,1,0:T(8,128)S(1)}, bf16[4096,256]{1,0:T(8,128)(2,1)S(1)}, bf16[4096,256]{1,0:T(8,128)(2,1)S(1)}) custom-call(s32[1]{0:T(128)S(6)} %copy.10.count.refs_0_, s32[1]{0:T(128)} %bitcast.refs_1_.place, s32[32]{0:T(128)S(1)} %copy-done.5, s32[32]{0:T(128)S(1)} %copy-done.4, ...), custom_call_target="tpu_custom_call" | custom-call | flops 3221225472 | bytes 4194304 | tf_op jit(solution)/shard_map/tiles/pallas_call | solution.py:281
  17.4 2.9 %collective-permute-start.3 = (f32[1,72,128]{2,1,0:T(8,128)S(1)}, f32[1,72,128]{2,1,0:T(8,128)S(1)}, u32[]{:S(2)}, u32[]{:S(2)}) collective-permute-start(f32[1,72,128]{2,1,0:T(8,128)S(1)} %bitcast.10), channel_id=1, source_target_pairs={{0,24},{1,25},{2,26},{3,27},{4,28},{5,29},{6,30},{7,31},{8,16},{9,... | collective-permute-start | bytes 110600 | tf_op jit(solution)/shard_map/ppermute | solution.py:239
  20.3 1.5 %collective-permute-start.5 = (f32[1,72,128]{2,1,0:T(8,128)S(1)}, f32[1,72,128]{2,1,0:T(8,128)S(1)}, u32[]{:S(2)}, u32[]{:S(2)}) collective-permute-start(f32[1,72,128]{2,1,0:T(8,128)S(1)} %bitcast.12), channel_id=1, source_target_pairs={{0,16},{1,17},{2,18},{3,19},{4,20},{5,21},{6,22},{7,23},{8,24},{9,... | collective-permute-start | bytes 110600 | tf_op jit(solution)/shard_map/ppermute | solution.py:239
  21.8 2.5 %tails.1 = f32[2,128,256]{2,1,0:T(8,128)S(1)} custom-call(s32[1]{0:T(128)} %bitcast.refs_1_.place, s32[32]{0:T(128)S(1)} %copy-done.5, f32[2,128,256]{2,1,0:T(8,128)S(1)} %get-tuple-element.22.heads, f32[32,256]{1,0:T(8,128)S(1)} %get-tuple-element.18.refs_10_.weights, bf16[4096,256]{1,0:T(8,128)(2,1)S(1)} %get-tuple-element.23.grads_high, ...), custom_call_target="tpu_custom_call" | custom-call | flops 1610612736 | bytes 4194304 | tf_op jit(solution)/shard_map/tails/pallas_call | solution.py:296
  24.4 0.9 %collective-permute-done.5 = f32[1,72,128]{2,1,0:T(8,128)S(1)} collective-permute-done((f32[1,72,128]{2,1,0:T(8,128)S(1)}, f32[1,72,128]{2,1,0:T(8,128)S(1)}, u32[]{:S(2)}, u32[]{:S(2)}) %collective-permute-start.5) | collective-permute-done | bytes 36896 | tf_op jit(solution)/shard_map/ppermute | solution.py:239
  25.3 2.3 %collective-permute-start.6 = (f32[4,72,128]{2,1,0:T(8,128)S(1)}, f32[4,72,128]{2,1,0:T(8,128)S(1)}, u32[]{:S(2)}, u32[]{:S(2)}) collective-permute-start(f32[4,72,128]{2,1,0:T(8,128)S(1)} %pad_maximum_fusion.1), channel_id=1, source_target_pairs={{0,5},{1,4},{2,7},{3,6},{4,1},{5,0},{6,3},{7,2},{8,13},{9,12},{10,... | collective-permute-start | bytes 442376 | tf_op jit(solution)/shard_map/ppermute | solution.py:239
  27.6 0.6 %collective-permute-start.7 = (f32[4,72,128]{2,1,0:T(8,128)S(1)}, f32[4,72,128]{2,1,0:T(8,128)S(1)}, u32[]{:S(2)}, u32[]{:S(2)}) collective-permute-start(f32[4,72,128]{2,1,0:T(8,128)S(1)} %pad_maximum_fusion.1), channel_id=1, source_target_pairs={{0,1},{1,0},{2,3},{3,2},{4,5},{5,4},{6,7},{7,6},{8,9},{9,8},{10,11... | collective-permute-start | bytes 442376 | tf_op jit(solution)/shard_map/ppermute | solution.py:239
  28.2 0.6 %collective-permute-start.8 = (f32[4,72,128]{2,1,0:T(8,128)S(1)}, f32[4,72,128]{2,1,0:T(8,128)S(1)}, u32[]{:S(2)}, u32[]{:S(2)}) collective-permute-start(f32[4,72,128]{2,1,0:T(8,128)S(1)} %pad_maximum_fusion.1), channel_id=1, source_target_pairs={{0,4},{1,5},{2,6},{3,7},{4,0},{5,1},{6,2},{7,3},{8,12},{9,13},{10,... | collective-permute-start | bytes 442376 | tf_op jit(solution)/shard_map/ppermute | solution.py:239
  28.8 0.3 collective-permute-start.9
  29.2 2.6 %collective-permute-done.6 = f32[4,72,128]{2,1,0:T(8,128)S(1)} collective-permute-done((f32[4,72,128]{2,1,0:T(8,128)S(1)}, f32[4,72,128]{2,1,0:T(8,128)S(1)}, u32[]{:S(2)}, u32[]{:S(2)}) %collective-permute-start.6) | collective-permute-done | bytes 147488 | tf_op jit(solution)/shard_map/ppermute | solution.py:239
  31.8 1.6 %collective-permute-done.7 = f32[4,72,128]{2,1,0:T(8,128)S(1)} collective-permute-done((f32[4,72,128]{2,1,0:T(8,128)S(1)}, f32[4,72,128]{2,1,0:T(8,128)S(1)}, u32[]{:S(2)}, u32[]{:S(2)}) %collective-permute-start.7) | collective-permute-done | bytes 147488 | tf_op jit(solution)/shard_map/ppermute | solution.py:239
  33.5 1.8 %collective-permute-done.8 = f32[4,72,128]{2,1,0:T(8,128)S(1)} collective-permute-done((f32[4,72,128]{2,1,0:T(8,128)S(1)}, f32[4,72,128]{2,1,0:T(8,128)S(1)}, u32[]{:S(2)}, u32[]{:S(2)}) %collective-permute-start.8) | collective-permute-done | bytes 147488 | tf_op jit(solution)/shard_map/ppermute | solution.py:239
  35.4 0.7 %collective-permute-start.10 = (f32[16,72,128]{2,1,0:T(8,128)S(1)}, f32[16,72,128]{2,1,0:T(8,128)S(1)}, u32[]{:S(2)}, u32[]{:S(2)}) collective-permute-start(f32[16,72,128]{2,1,0:T(8,128)S(1)} %pad_maximum_fusion.held), channel_id=1, source_target_pairs={{0,2},{1,3},{2,0},{3,1},{4,6},{5,7},{6,4},{7,5},{8,10},{9,11},{10,... | collective-permute-start | bytes 1769480 | tf_op jit(solution)/shard_map/ppermute | solution.py:324
  36.1 1.7 %collective-permute-start.11 = (f32[128,256]{1,0:T(8,128)S(1)}, f32[128,256]{1,0:T(8,128)S(1)}, u32[]{:S(2)}, u32[]{:S(2)}) collective-permute-start(f32[128,256]{1,0:T(8,128)S(1)} %get-tuple-element.34), channel_id=1, source_target_pairs={{0,1},{1,0},{2,3},{3,2},{4,5},{5,4},{6,7},{7,6},{8,9},{9,8},{10,11... | collective-permute-start | bytes 393224 | tf_op jit(solution)/shard_map/ppermute | solution.py:230
  37.8 0.6 %combine.2.before = f32[900,256]{1,0:T(8,128)S(1)} custom-call(f32[16,72,128]{2,1,0:T(8,128)S(1)} %pad_maximum_fusion.held), custom_call_target="tpu_custom_call" | custom-call | flops 471859200 | bytes 2097152 | tf_op jit(solution)/shard_map/combine/pallas_call | solution.py:208
  38.4 1.6 %combine.3 = f32[900,256]{1,0:T(8,128)} custom-call(f32[16,72,128]{2,1,0:T(8,128)S(1)} %collective-permute-done.10.gathered, f32[900,256]{1,0:T(8,128)S(1)} %combine.2.before), custom_call_target="tpu_custom_call" | custom-call | flops 471859200 | bytes 2097152 | tf_op jit(solution)/shard_map/combine/pallas_call | solution.py:208
  40.0 1.5 %collective-permute-done.11 = f32[128,256]{1,0:T(8,128)S(1)} collective-permute-done((f32[128,256]{1,0:T(8,128)S(1)}, f32[128,256]{1,0:T(8,128)S(1)}, u32[]{:S(2)}, u32[]{:S(2)}) %collective-permute-start.11) | collective-permute-done | bytes 131104 | tf_op jit(solution)/shard_map/ppermute | solution.py:230
  41.6 0.7 %add.31 = f32[128,256]{1,0:T(8,128)} add(f32[128,256]{1,0:T(8,128)S(1)} %get-tuple-element.29, f32[128,256]{1,0:T(8,128)S(1)} %collective-permute-done.11) | non-fusion elementwise | flops 32768 | bytes 393216 | tf_op jit(solution)/shard_map/add | solution.py:330
  (24 shorter events, 0.2 us)
Async XLA Ops:
  0.6 9.4 %collective-permute-start = (f32[128,256]{1,0:T(8,128)}, f32[128,256]{1,0:T(8,128)S(1)}, u32[]{:S(2)}, u32[]{:S(2)}) collective-permute-start(f32[128,256]{1,0:T(8,128)} %entity.1), channel_id=1, source_target_pairs={{0,3},{1,2},{2,5},{3,4},{4,7},{5,6},{6,9},{7,8},{8,11},{9,10},{10,... | collective-permute-start | bytes 393224 | tf_op jit(solution)/shard_map/ppermute | solution.py:230
  3.1 8.7 %collective-permute-start.1 = (f32[128,256]{1,0:T(8,128)}, f32[128,256]{1,0:T(8,128)S(1)}, u32[]{:S(2)}, u32[]{:S(2)}) collective-permute-start(f32[128,256]{1,0:T(8,128)} %entity.1), channel_id=1, source_target_pairs={{0,2},{1,3},{2,4},{3,5},{4,6},{5,7},{6,8},{7,9},{8,10},{9,11},{10,... | collective-permute-start | bytes 393224 | tf_op jit(solution)/shard_map/ppermute | solution.py:230
  4.7 7.1 %collective-permute-start.2 = (f32[128,256]{1,0:T(8,128)}, f32[128,256]{1,0:T(8,128)}, u32[]{:S(2)}, u32[]{:S(2)}) collective-permute-start(f32[128,256]{1,0:T(8,128)} %entity.1), channel_id=1, source_target_pairs={{0,1},{1,0},{2,3},{3,2},{4,5},{5,4},{6,7},{7,6},{8,9},{9,8},{10,11... | collective-permute-start | bytes 393224 | tf_op jit(solution)/shard_map/ppermute | solution.py:230
  5.9 1.9 %copy-start = (f32[900,256]{1,0:T(8,128)S(1)}, f32[900,256]{1,0:T(8,128)}, u32[]{:S(2)}) copy-start(f32[900,256]{1,0:T(8,128)} %rel_weight.1) | copy-start | bytes 2764804
  5.9 1.9 %copy-start.1 = (f32[128,256]{1,0:T(8,128)S(1)}, f32[128,256]{1,0:T(8,128)}, u32[]{:S(2)}) copy-start(f32[128,256]{1,0:T(8,128)} %entity.1) | copy-start | bytes 393220
  5.9 1.9 %copy-start.2 = (s32[32,256]{1,0:T(8,128)S(1)}, s32[32,256]{1,0:T(8,128)}, u32[]{:S(2)}) copy-start(s32[32,256]{1,0:T(8,128)} %negatives.1) | copy-start | bytes 98308
  5.9 1.9 %copy-start.3 = (s32[32]{0:T(128)S(1)}, s32[32]{0:T(128)}, u32[]{:S(2)}) copy-start(s32[32]{0:T(128)} %rel_ids.1) | copy-start | bytes 388
  5.9 5.9 %copy-start.4 = (s32[32]{0:T(128)S(1)}, s32[32]{0:T(128)}, u32[]{:S(2)}) copy-start(s32[32]{0:T(128)} %refs_3_.1) | copy-start | bytes 388
  5.9 5.9 %copy-start.5 = (s32[32]{0:T(128)S(1)}, s32[32]{0:T(128)}, u32[]{:S(2)}) copy-start(s32[32]{0:T(128)} %head_in_ids.1) | copy-start | bytes 388
  17.4 7.0 %collective-permute-start.3 = (f32[1,72,128]{2,1,0:T(8,128)S(1)}, f32[1,72,128]{2,1,0:T(8,128)S(1)}, u32[]{:S(2)}, u32[]{:S(2)}) collective-permute-start(f32[1,72,128]{2,1,0:T(8,128)S(1)} %bitcast.10), channel_id=1, source_target_pairs={{0,24},{1,25},{2,26},{3,27},{4,28},{5,29},{6,30},{7,31},{8,16},{9,... | collective-permute-start | bytes 110600 | tf_op jit(solution)/shard_map/ppermute | solution.py:239
  20.3 4.1 %collective-permute-start.4 = (f32[1,72,128]{2,1,0:T(8,128)S(1)}, f32[1,72,128]{2,1,0:T(8,128)S(1)}, u32[]{:S(2)}, u32[]{:S(2)}) collective-permute-start(f32[1,72,128]{2,1,0:T(8,128)S(1)} %bitcast.11), channel_id=1, source_target_pairs={{0,8},{1,9},{2,10},{3,11},{4,12},{5,13},{6,14},{7,15},{8,0},{9,1},... | collective-permute-start | bytes 110600 | tf_op jit(solution)/shard_map/ppermute | solution.py:239
  20.3 4.9 %collective-permute-start.5 = (f32[1,72,128]{2,1,0:T(8,128)S(1)}, f32[1,72,128]{2,1,0:T(8,128)S(1)}, u32[]{:S(2)}, u32[]{:S(2)}) collective-permute-start(f32[1,72,128]{2,1,0:T(8,128)S(1)} %bitcast.12), channel_id=1, source_target_pairs={{0,16},{1,17},{2,18},{3,19},{4,20},{5,21},{6,22},{7,23},{8,24},{9,... | collective-permute-start | bytes 110600 | tf_op jit(solution)/shard_map/ppermute | solution.py:239
  25.3 6.5 %collective-permute-start.6 = (f32[4,72,128]{2,1,0:T(8,128)S(1)}, f32[4,72,128]{2,1,0:T(8,128)S(1)}, u32[]{:S(2)}, u32[]{:S(2)}) collective-permute-start(f32[4,72,128]{2,1,0:T(8,128)S(1)} %pad_maximum_fusion.1), channel_id=1, source_target_pairs={{0,5},{1,4},{2,7},{3,6},{4,1},{5,0},{6,3},{7,2},{8,13},{9,12},{10,... | collective-permute-start | bytes 442376 | tf_op jit(solution)/shard_map/ppermute | solution.py:239
  27.6 5.9 %collective-permute-start.7 = (f32[4,72,128]{2,1,0:T(8,128)S(1)}, f32[4,72,128]{2,1,0:T(8,128)S(1)}, u32[]{:S(2)}, u32[]{:S(2)}) collective-permute-start(f32[4,72,128]{2,1,0:T(8,128)S(1)} %pad_maximum_fusion.1), channel_id=1, source_target_pairs={{0,1},{1,0},{2,3},{3,2},{4,5},{5,4},{6,7},{7,6},{8,9},{9,8},{10,11... | collective-permute-start | bytes 442376 | tf_op jit(solution)/shard_map/ppermute | solution.py:239
  28.2 7.0 %collective-permute-start.8 = (f32[4,72,128]{2,1,0:T(8,128)S(1)}, f32[4,72,128]{2,1,0:T(8,128)S(1)}, u32[]{:S(2)}, u32[]{:S(2)}) collective-permute-start(f32[4,72,128]{2,1,0:T(8,128)S(1)} %pad_maximum_fusion.1), channel_id=1, source_target_pairs={{0,4},{1,5},{2,6},{3,7},{4,0},{5,1},{6,2},{7,3},{8,12},{9,13},{10,... | collective-permute-start | bytes 442376 | tf_op jit(solution)/shard_map/ppermute | solution.py:239
  28.8 6.5 %collective-permute-start.9 = (f32[2,128,256]{2,1,0:T(8,128)S(1)}, f32[2,128,256]{2,1,0:T(8,128)S(1)}, u32[]{:S(2)}, u32[]{:S(2)}) collective-permute-start(f32[2,128,256]{2,1,0:T(8,128)S(1)} %tails.1), channel_id=1, source_target_pairs={{0,30},{1,31},{2,0},{3,1},{4,2},{5,3},{6,4},{7,5},{8,6},{9,7},{10,... | collective-permute-start | bytes 786440 | tf_op jit(solution)/shard_map/ppermute | solution.py:230
  35.4 3.1 %collective-permute-start.10 = (f32[16,72,128]{2,1,0:T(8,128)S(1)}, f32[16,72,128]{2,1,0:T(8,128)S(1)}, u32[]{:S(2)}, u32[]{:S(2)}) collective-permute-start(f32[16,72,128]{2,1,0:T(8,128)S(1)} %pad_maximum_fusion.held), channel_id=1, source_target_pairs={{0,2},{1,3},{2,0},{3,1},{4,6},{5,7},{6,4},{7,5},{8,10},{9,11},{10,... | collective-permute-start | bytes 1769480 | tf_op jit(solution)/shard_map/ppermute | solution.py:324
  36.1 5.5 %collective-permute-start.11 = (f32[128,256]{1,0:T(8,128)S(1)}, f32[128,256]{1,0:T(8,128)S(1)}, u32[]{:S(2)}, u32[]{:S(2)}) collective-permute-start(f32[128,256]{1,0:T(8,128)S(1)} %get-tuple-element.34), channel_id=1, source_target_pairs={{0,1},{1,0},{2,3},{3,2},{4,5},{5,4},{6,7},{7,6},{8,9},{9,8},{10,11... | collective-permute-start | bytes 393224 | tf_op jit(solution)/shard_map/ppermute | solution.py:230

commit v5 on v4

--- a/solution.py
+++ b/solution.py
@@ -143,7 +143,8 @@
         head_out[k] = head_grad[mine ^ k]
 
 
-def tails_kernel(place, head_in_ids, heads, weights, grads_high, grads_low, tail_out, tail_grad, head_ids, sem):
+def tails_kernel(place, head_in_ids, head_parts, heads, weights, grads_high, grads_low, *refs):
+    pairs_out, (tail_grad, head_ids, sem) = refs[:-3], refs[-3:]
     blocks, block, _ = heads.shape
     tiles = weights.shape[0]
     copy = pltpu.make_async_copy(head_in_ids, head_ids, sem)
@@ -160,7 +161,8 @@
         else:
             tail_grad[...] += part
     for k in range(blocks):
-        tail_out[k] = tail_grad[place[0] ^ k]
+        pairs_out[k][0] = head_parts[k]
+        pairs_out[k][1] = tail_grad[place[0] ^ k]
 
 
 def combine_kernel(gathered, before, out):
@@ -293,11 +295,11 @@
         ),
         name="tiles",
     )(tile_count, place, tile_head, tile_tail, *tails[::-1], own, *others, mask, counts, weights, names)
-    tail_parts = pl.pallas_call(
+    pairs = pl.pallas_call(
         tails_kernel,
-        out_shape=pieces,
-        in_specs=[smem, spec(pl.ANY)] + [vmem] * 4,
-        out_specs=vmem,
+        out_shape=[jax.ShapeDtypeStruct((2, block, width), F32)] * reps,
+        in_specs=[smem, spec(pl.ANY)] + [vmem] * 5,
+        out_specs=[vmem] * reps,
         scratch_shapes=[
             pltpu.VMEM((reps, block, width), F32),
             pltpu.SMEM((tiles,), jnp.int32),
@@ -308,27 +310,28 @@
             flops=6 * tiles * block * partition * width, bytes_accessed=4 << 20, transcendentals=0
         ),
         name="tails",
-    )(place, tile_head, heads, weights, grads_high, grads_low)
+    )(place, tile_head, head_parts, heads, weights, grads_high, grads_low)
 
     total = shards * reps
     low = reps.bit_length() - 1
     top = total.bit_length() - 1
-    order = list(range(top - 1, low, -1)) + list(range(low - 1, -1, -1))
+    order = [top - 1, *range(low - 1, -1, -1), *range(top - 2, low, -1)]
     index = lax.axis_index("shard") * reps + lax.axis_index("rep")
     held = exchange(terms[None], order[:2], index, total)
-    held, tail_parts = lax.optimization_barrier((held, tail_parts))
-    returned = permute(tail_parts, shards, reps, -1, 0)
+    held, pairs = lax.optimization_barrier((held, pairs))
+    arrived = [permute(pairs[k], shards, reps, 0, k) for k in range(1, reps)]
     for i in range(2, len(order), 2):
         held = exchange(held, order[i : i + 2], index, total)
-    held, returned = lax.optimization_barrier((held, returned))
+    held, arrived = lax.optimization_barrier((held, arrived))
     theirs = lax.ppermute(held, AXES, [(d, d ^ (1 << low)) for d in range(total)])
-    arrived = [permute(head_parts[k] + returned[k], shards, reps, 0, k) for k in range(1, reps)]
+    summed = pairs[0]
+    for part in arrived:
+        summed = summed + part
+    returned = permute(summed[1], shards, reps, -1, 0)
     half = combine(held, rels, width)
     rel_grad = combine(theirs, rels, width, half)
-    entity_grad, _ = lax.optimization_barrier((head_parts[0] + returned[0], rel_grad))
-    for part in arrived:
-        entity_grad = entity_grad + part
-    return (entity_grad, rel_grad)
+    entity_grad, _ = lax.optimization_barrier((summed[0], rel_grad))
+    return (entity_grad + returned, rel_grad)
 
 
 def solution(mesh):

time: 42.4 us -> 41.7 us (0.983)
  waiting for transfers between devices: 10.2 us -> 8.42 us
  starting transfers between devices: 15.3 us -> 16.5 us
    ppermute x6, waiting for transfers between devices: 6.96 us -> 5.05 us  [exchange(): lax.ppermute(held, AXES, [(d, d ^ flip) for d in range(total)])]
    ppermute x5, starting transfers between devices: 6.65 us -> 8.5 us  [permute(): return lax.ppermute(value, AXES, route)]
    ppermute x1, starting transfers between devices: 0.66 us -> 0.01 us  [local(): theirs = lax.ppermute(held, AXES, [(d, d ^ 1 << low) for d in range(total)])]
where the time goes in v5:
time: 41.7 us; the launch traced here: 41.5 us
  starting transfers between devices  16.5 us (40%)
  Pallas kernels  12.4 us (30%)
  waiting for transfers between devices  8.42 us (20%)
  other arithmetic  2.64 us (6%)
  between operations  1.48 us (4%)
    ppermute x5, starting transfers between devices, permute(): return lax.ppermute(value, AXES, route)  8.5 us
    ppermute x6, starting transfers between devices, exchange(): lax.ppermute(held, AXES, [(d, d ^ flip) for d in range(total)])  8.01 us
    pallas_call x1, Pallas kernels, local(): pl.pallas_call(functools.partial(tiles_kernel, reps), out_shape=[jax.Shap...  5.5 us
    ppermute x6, waiting for transfers between devices, exchange(): lax.ppermute(held, AXES, [(d, d ^ flip) for d in range(total)])  5.05 us
    ppermute x5, waiting for transfers between devices, permute(): return lax.ppermute(value, AXES, route)  3.37 us
    pallas_call x1, Pallas kernels, local(): pl.pallas_call(tails_kernel, out_shape=[jax.ShapeDtypeStruct((2, block, w...  2.49 us
    pallas_call x1, Pallas kernels, local(): pl.pallas_call(prepare_kernel, out_shape=(jax.ShapeDtypeStruct((tiles, pa...  2.24 us
    pallas_call x2, Pallas kernels, combine(): pl.pallas_call(kernel, out_shape=jax.ShapeDtypeStruct((rels, width), F32)...  2.23 us
  transfers between devices with their start and end apart: 12, of which 6 were waited for; matrix products, arithmetic and copies ran while one was open for 5% of the time, Pallas kernels for 17%

profile of v5, /device:TPU:0, one launch (start us, length us, event | category | flops | bytes accessed | tf_op | source)
XLA Modules:
  0.0 41.5 jit_solution(13947367557355214282)
XLA Ops:
  0.6 2.4 %collective-permute-start = (f32[128,256]{1,0:T(8,128)}, f32[128,256]{1,0:T(8,128)S(1)}, u32[]{:S(2)}, u32[]{:S(2)}) collective-permute-start(f32[128,256]{1,0:T(8,128)} %entity.1), channel_id=1, source_target_pairs={{0,3},{1,2},{2,5},{3,4},{4,7},{5,6},{6,9},{7,8},{8,11},{9,10},{10,... | collective-permute-start | bytes 393224 | tf_op jit(solution)/shard_map/ppermute | solution.py:232
  3.1 1.6 %collective-permute-start.1 = (f32[128,256]{1,0:T(8,128)}, f32[128,256]{1,0:T(8,128)S(1)}, u32[]{:S(2)}, u32[]{:S(2)}) collective-permute-start(f32[128,256]{1,0:T(8,128)} %entity.1), channel_id=1, source_target_pairs={{0,2},{1,3},{2,4},{3,5},{4,6},{5,7},{6,8},{7,9},{8,10},{9,11},{10,... | collective-permute-start | bytes 393224 | tf_op jit(solution)/shard_map/ppermute | solution.py:232
  4.7 0.5 %collective-permute-start.2 = (f32[128,256]{1,0:T(8,128)}, f32[128,256]{1,0:T(8,128)}, u32[]{:S(2)}, u32[]{:S(2)}) collective-permute-start(f32[128,256]{1,0:T(8,128)} %entity.1), channel_id=1, source_target_pairs={{0,1},{1,0},{2,3},{3,2},{4,5},{5,4},{6,7},{7,6},{8,9},{9,8},{10,11... | collective-permute-start | bytes 393224 | tf_op jit(solution)/shard_map/ppermute | solution.py:232
  5.9 1.8 %convert_element_type.3.refs_8_ = f32[32,128,128]{2,1,0:T(8,128)S(1)} convert(s32[32,128,128]{2,1,0:T(8,128)} %param.13) | non-fusion elementwise | flops 524288 | bytes 4194304 | tf_op jit(solution)/shard_map/convert_element_type | solution.py:279
  7.8 2.2 %prepare.1 = (f32[32,256]{1,0:T(8,128)S(1)}, f32[32,256]{1,0:T(8,128)S(1)}, f32[1,128]{1,0:T(1,128)S(1)}, f32[128,256]{1,0:T(8,128)S(1)}) custom-call(s32[1]{0:T(128)S(6)} %copy.10.count.refs_0_, s32[32]{0:T(128)S(1)} %copy-done.3, s32[32,256]{1,0:T(8,128)S(1)} %copy-done.2, f32[900,256]{1,0:T(8,128)S(1)} %copy-done, f32[128,256]{1,0:T(8,128)S(1)} %copy-done.1), custom_call_target="tpu_custom_call" | custom-call | flops 4194304 | bytes 4194304 | tf_op jit(solution)/shard_map/prepare/pallas_call | solution.py:259
  10.1 1.8 %collective-permute-done.1.refs_5_ = f32[128,256]{1,0:T(8,128)S(1)} collective-permute-done((f32[128,256]{1,0:T(8,128)}, f32[128,256]{1,0:T(8,128)S(1)}, u32[]{:S(2)}, u32[]{:S(2)}) %collective-permute-start.1) | collective-permute-done | bytes 131104 | tf_op jit(solution)/shard_map/ppermute | solution.py:232
  11.8 5.5 %tiles.1 = (f32[72,128]{1,0:T(8,128)S(1)}, f32[2,128,256]{2,1,0:T(8,128)S(1)}, f32[2,128,256]{2,1,0:T(8,128)S(1)}, bf16[4096,256]{1,0:T(8,128)(2,1)S(1)}, bf16[4096,256]{1,0:T(8,128)(2,1)S(1)}) custom-call(s32[1]{0:T(128)S(6)} %copy.10.count.refs_0_, s32[1]{0:T(128)} %bitcast.refs_1_.place, s32[32]{0:T(128)S(1)} %copy-done.5, s32[32]{0:T(128)S(1)} %copy-done.4, ...), custom_call_target="tpu_custom_call" | custom-call | flops 3221225472 | bytes 4194304 | tf_op jit(solution)/shard_map/tiles/pallas_call | solution.py:283
  17.3 2.2 %collective-permute-start.3 = (f32[1,72,128]{2,1,0:T(8,128)S(1)}, f32[1,72,128]{2,1,0:T(8,128)S(1)}, u32[]{:S(2)}, u32[]{:S(2)}) collective-permute-start(f32[1,72,128]{2,1,0:T(8,128)S(1)} %bitcast.10), channel_id=1, source_target_pairs={{0,17},{1,16},{2,19},{3,18},{4,21},{5,20},{6,23},{7,22},{8,25},{9,... | collective-permute-start | bytes 110600 | tf_op jit(solution)/shard_map/ppermute | solution.py:241
  19.5 1.2 %collective-permute-start.4 = (f32[1,72,128]{2,1,0:T(8,128)S(1)}, f32[1,72,128]{2,1,0:T(8,128)S(1)}, u32[]{:S(2)}, u32[]{:S(2)}) collective-permute-start(f32[1,72,128]{2,1,0:T(8,128)S(1)} %bitcast.11), channel_id=1, source_target_pairs={{0,1},{1,0},{2,3},{3,2},{4,5},{5,4},{6,7},{7,6},{8,9},{9,8},{10,11... | collective-permute-start | bytes 110600 | tf_op jit(solution)/shard_map/ppermute | solution.py:241
  20.7 1.1 %collective-permute-start.5 = (f32[1,72,128]{2,1,0:T(8,128)S(1)}, f32[1,72,128]{2,1,0:T(8,128)S(1)}, u32[]{:S(2)}, u32[]{:S(2)}) collective-permute-start(f32[1,72,128]{2,1,0:T(8,128)S(1)} %bitcast.12), channel_id=1, source_target_pairs={{0,16},{1,17},{2,18},{3,19},{4,20},{5,21},{6,22},{7,23},{8,24},{9,... | collective-permute-start | bytes 110600 | tf_op jit(solution)/shard_map/ppermute | solution.py:241
  21.8 2.5 %tails.1 = (f32[2,128,256]{2,1,0:T(8,128)S(1)}, f32[2,128,256]{2,1,0:T(8,128)S(1)}) custom-call(s32[1]{0:T(128)} %bitcast.refs_1_.place, s32[32]{0:T(128)S(1)} %copy-done.5, f32[2,128,256]{2,1,0:T(8,128)S(1)} %get-tuple-element.24.head_parts, f32[2,128,256]{2,1,0:T(8,128)S(1)} %get-tuple-element.25.heads, f32[32,256]{1,0:T(8,128)S(1)} %get-tuple-element.21.refs_10_.weights, ...), custom_call_target="tpu_custom_call" | custom-call | flops 1610612736 | bytes 4194304 | tf_op jit(solution)/shard_map/tails/pallas_call | solution.py:298
  24.3 1.3 %collective-permute-done.5 = f32[1,72,128]{2,1,0:T(8,128)S(1)} collective-permute-done((f32[1,72,128]{2,1,0:T(8,128)S(1)}, f32[1,72,128]{2,1,0:T(8,128)S(1)}, u32[]{:S(2)}, u32[]{:S(2)}) %collective-permute-start.5) | collective-permute-done | bytes 36896 | tf_op jit(solution)/shard_map/ppermute | solution.py:241
  25.6 2.6 %collective-permute-start.6 = (f32[4,72,128]{2,1,0:T(8,128)S(1)}, f32[4,72,128]{2,1,0:T(8,128)S(1)}, u32[]{:S(2)}, u32[]{:S(2)}) collective-permute-start(f32[4,72,128]{2,1,0:T(8,128)S(1)} %pad_maximum_fusion.1), channel_id=1, source_target_pairs={{0,12},{1,13},{2,14},{3,15},{4,8},{5,9},{6,10},{7,11},{8,4},{9,5},... | collective-permute-start | bytes 442376 | tf_op jit(solution)/shard_map/ppermute | solution.py:241
  28.2 0.5 %collective-permute-start.7 = (f32[4,72,128]{2,1,0:T(8,128)S(1)}, f32[4,72,128]{2,1,0:T(8,128)S(1)}, u32[]{:S(2)}, u32[]{:S(2)}) collective-permute-start(f32[4,72,128]{2,1,0:T(8,128)S(1)} %pad_maximum_fusion.1), channel_id=1, source_target_pairs={{0,4},{1,5},{2,6},{3,7},{4,0},{5,1},{6,2},{7,3},{8,12},{9,13},{10,... | collective-permute-start | bytes 442376 | tf_op jit(solution)/shard_map/ppermute | solution.py:241
  28.7 0.4 %collective-permute-start.8 = (f32[4,72,128]{2,1,0:T(8,128)S(1)}, f32[4,72,128]{2,1,0:T(8,128)S(1)}, u32[]{:S(2)}, u32[]{:S(2)}) collective-permute-start(f32[4,72,128]{2,1,0:T(8,128)S(1)} %pad_maximum_fusion.1), channel_id=1, source_target_pairs={{0,8},{1,9},{2,10},{3,11},{4,12},{5,13},{6,14},{7,15},{8,0},{9,1},... | collective-permute-start | bytes 442376 | tf_op jit(solution)/shard_map/ppermute | solution.py:241
  29.2 1.2 %collective-permute-start.9 = (f32[2,128,256]{2,1,0:T(8,128)S(1)}, f32[2,128,256]{2,1,0:T(8,128)S(1)}, u32[]{:S(2)}, u32[]{:S(2)}) collective-permute-start(f32[2,128,256]{2,1,0:T(8,128)S(1)} %get-tuple-element.32), channel_id=1, source_target_pairs={{0,1},{1,0},{2,3},{3,2},{4,5},{5,4},{6,7},{7,6},{8,9},{9,8},{10,11... | collective-permute-start | bytes 786440 | tf_op jit(solution)/shard_map/ppermute | solution.py:232
  30.3 2.3 %collective-permute-done.6 = f32[4,72,128]{2,1,0:T(8,128)S(1)} collective-permute-done((f32[4,72,128]{2,1,0:T(8,128)S(1)}, f32[4,72,128]{2,1,0:T(8,128)S(1)}, u32[]{:S(2)}, u32[]{:S(2)}) %collective-permute-start.6) | collective-permute-done | bytes 147488 | tf_op jit(solution)/shard_map/ppermute | solution.py:241
  32.7 1.4 %collective-permute-done.7 = f32[4,72,128]{2,1,0:T(8,128)S(1)} collective-permute-done((f32[4,72,128]{2,1,0:T(8,128)S(1)}, f32[4,72,128]{2,1,0:T(8,128)S(1)}, u32[]{:S(2)}, u32[]{:S(2)}) %collective-permute-start.7) | collective-permute-done | bytes 147488 | tf_op jit(solution)/shard_map/ppermute | solution.py:241
  34.2 1.3 %collective-permute-done.9 = f32[2,128,256]{2,1,0:T(8,128)S(1)} collective-permute-done((f32[2,128,256]{2,1,0:T(8,128)S(1)}, f32[2,128,256]{2,1,0:T(8,128)S(1)}, u32[]{:S(2)}, u32[]{:S(2)}) %collective-permute-start.9) | collective-permute-done | bytes 262176 | tf_op jit(solution)/shard_map/ppermute | solution.py:232
  35.6 2.7 %collective-permute-start.11 = (f32[128,256]{1,0:T(8,128)S(1)}, f32[128,256]{1,0:T(8,128)S(1)}, u32[]{:S(2)}, u32[]{:S(2)}) collective-permute-start(f32[128,256]{1,0:T(8,128)S(1)} %get-tuple-element.40), channel_id=1, source_target_pairs={{0,30},{1,31},{2,0},{3,1},{4,2},{5,3},{6,4},{7,5},{8,6},{9,7},{10,... | collective-permute-start | bytes 393224 | tf_op jit(solution)/shard_map/ppermute | solution.py:232
  38.4 0.6 %combine.2.before = f32[900,256]{1,0:T(8,128)S(1)} custom-call(f32[16,72,128]{2,1,0:T(8,128)S(1)} %pad_maximum_fusion.held), custom_call_target="tpu_custom_call" | custom-call | flops 471859200 | bytes 2097152 | tf_op jit(solution)/shard_map/combine/pallas_call | solution.py:210
  39.0 1.6 %combine.3 = f32[900,256]{1,0:T(8,128)} custom-call(f32[16,72,128]{2,1,0:T(8,128)S(1)} %collective-permute-done.10.gathered, f32[900,256]{1,0:T(8,128)S(1)} %combine.2.before), custom_call_target="tpu_custom_call" | custom-call | flops 471859200 | bytes 2097152 | tf_op jit(solution)/shard_map/combine/pallas_call | solution.py:210
  40.6 0.3 collective-permute-done.11
  40.9 0.7 %add.19 = f32[128,256]{1,0:T(8,128)} add(f32[128,256]{1,0:T(8,128)S(1)} %get-tuple-element.35, f32[128,256]{1,0:T(8,128)S(1)} %collective-permute-done.11) | non-fusion elementwise | flops 32768 | bytes 393216 | tf_op jit(solution)/shard_map/add | solution.py:334
  (25 shorter events, 0.2 us)
Async XLA Ops:
  0.6 9.4 %collective-permute-start = (f32[128,256]{1,0:T(8,128)}, f32[128,256]{1,0:T(8,128)S(1)}, u32[]{:S(2)}, u32[]{:S(2)}) collective-permute-start(f32[128,256]{1,0:T(8,128)} %entity.1), channel_id=1, source_target_pairs={{0,3},{1,2},{2,5},{3,4},{4,7},{5,6},{6,9},{7,8},{8,11},{9,10},{10,... | collective-permute-start | bytes 393224 | tf_op jit(solution)/shard_map/ppermute | solution.py:232
  3.1 8.7 %collective-permute-start.1 = (f32[128,256]{1,0:T(8,128)}, f32[128,256]{1,0:T(8,128)S(1)}, u32[]{:S(2)}, u32[]{:S(2)}) collective-permute-start(f32[128,256]{1,0:T(8,128)} %entity.1), channel_id=1, source_target_pairs={{0,2},{1,3},{2,4},{3,5},{4,6},{5,7},{6,8},{7,9},{8,10},{9,11},{10,... | collective-permute-start | bytes 393224 | tf_op jit(solution)/shard_map/ppermute | solution.py:232
  4.7 7.1 %collective-permute-start.2 = (f32[128,256]{1,0:T(8,128)}, f32[128,256]{1,0:T(8,128)}, u32[]{:S(2)}, u32[]{:S(2)}) collective-permute-start(f32[128,256]{1,0:T(8,128)} %entity.1), channel_id=1, source_target_pairs={{0,1},{1,0},{2,3},{3,2},{4,5},{5,4},{6,7},{7,6},{8,9},{9,8},{10,11... | collective-permute-start | bytes 393224 | tf_op jit(solution)/shard_map/ppermute | solution.py:232
  5.9 1.9 %copy-start = (f32[900,256]{1,0:T(8,128)S(1)}, f32[900,256]{1,0:T(8,128)}, u32[]{:S(2)}) copy-start(f32[900,256]{1,0:T(8,128)} %rel_weight.1) | copy-start | bytes 2764804
  5.9 1.9 %copy-start.1 = (f32[128,256]{1,0:T(8,128)S(1)}, f32[128,256]{1,0:T(8,128)}, u32[]{:S(2)}) copy-start(f32[128,256]{1,0:T(8,128)} %entity.1) | copy-start | bytes 393220
  5.9 1.9 %copy-start.2 = (s32[32,256]{1,0:T(8,128)S(1)}, s32[32,256]{1,0:T(8,128)}, u32[]{:S(2)}) copy-start(s32[32,256]{1,0:T(8,128)} %negatives.1) | copy-start | bytes 98308
  5.9 1.9 %copy-start.3 = (s32[32]{0:T(128)S(1)}, s32[32]{0:T(128)}, u32[]{:S(2)}) copy-start(s32[32]{0:T(128)} %rel_ids.1) | copy-start | bytes 388
  5.9 5.9 %copy-start.4 = (s32[32]{0:T(128)S(1)}, s32[32]{0:T(128)}, u32[]{:S(2)}) copy-start(s32[32]{0:T(128)} %refs_3_.1) | copy-start | bytes 388
  5.9 5.9 %copy-start.5 = (s32[32]{0:T(128)S(1)}, s32[32]{0:T(128)}, u32[]{:S(2)}) copy-start(s32[32]{0:T(128)} %head_in_ids.1) | copy-start | bytes 388
  17.3 7.0 %collective-permute-start.3 = (f32[1,72,128]{2,1,0:T(8,128)S(1)}, f32[1,72,128]{2,1,0:T(8,128)S(1)}, u32[]{:S(2)}, u32[]{:S(2)}) collective-permute-start(f32[1,72,128]{2,1,0:T(8,128)S(1)} %bitcast.10), channel_id=1, source_target_pairs={{0,17},{1,16},{2,19},{3,18},{4,21},{5,20},{6,23},{7,22},{8,25},{9,... | collective-permute-start | bytes 110600 | tf_op jit(solution)/shard_map/ppermute | solution.py:241
  19.5 4.8 %collective-permute-start.4 = (f32[1,72,128]{2,1,0:T(8,128)S(1)}, f32[1,72,128]{2,1,0:T(8,128)S(1)}, u32[]{:S(2)}, u32[]{:S(2)}) collective-permute-start(f32[1,72,128]{2,1,0:T(8,128)S(1)} %bitcast.11), channel_id=1, source_target_pairs={{0,1},{1,0},{2,3},{3,2},{4,5},{5,4},{6,7},{7,6},{8,9},{9,8},{10,11... | collective-permute-start | bytes 110600 | tf_op jit(solution)/shard_map/ppermute | solution.py:241
  20.7 4.9 %collective-permute-start.5 = (f32[1,72,128]{2,1,0:T(8,128)S(1)}, f32[1,72,128]{2,1,0:T(8,128)S(1)}, u32[]{:S(2)}, u32[]{:S(2)}) collective-permute-start(f32[1,72,128]{2,1,0:T(8,128)S(1)} %bitcast.12), channel_id=1, source_target_pairs={{0,16},{1,17},{2,18},{3,19},{4,20},{5,21},{6,22},{7,23},{8,24},{9,... | collective-permute-start | bytes 110600 | tf_op jit(solution)/shard_map/ppermute | solution.py:241
  25.6 7.0 %collective-permute-start.6 = (f32[4,72,128]{2,1,0:T(8,128)S(1)}, f32[4,72,128]{2,1,0:T(8,128)S(1)}, u32[]{:S(2)}, u32[]{:S(2)}) collective-permute-start(f32[4,72,128]{2,1,0:T(8,128)S(1)} %pad_maximum_fusion.1), channel_id=1, source_target_pairs={{0,12},{1,13},{2,14},{3,15},{4,8},{5,9},{6,10},{7,11},{8,4},{9,5},... | collective-permute-start | bytes 442376 | tf_op jit(solution)/shard_map/ppermute | solution.py:241
  28.2 5.9 %collective-permute-start.7 = (f32[4,72,128]{2,1,0:T(8,128)S(1)}, f32[4,72,128]{2,1,0:T(8,128)S(1)}, u32[]{:S(2)}, u32[]{:S(2)}) collective-permute-start(f32[4,72,128]{2,1,0:T(8,128)S(1)} %pad_maximum_fusion.1), channel_id=1, source_target_pairs={{0,4},{1,5},{2,6},{3,7},{4,0},{5,1},{6,2},{7,3},{8,12},{9,13},{10,... | collective-permute-start | bytes 442376 | tf_op jit(solution)/shard_map/ppermute | solution.py:241
  28.7 5.4 %collective-permute-start.8 = (f32[4,72,128]{2,1,0:T(8,128)S(1)}, f32[4,72,128]{2,1,0:T(8,128)S(1)}, u32[]{:S(2)}, u32[]{:S(2)}) collective-permute-start(f32[4,72,128]{2,1,0:T(8,128)S(1)} %pad_maximum_fusion.1), channel_id=1, source_target_pairs={{0,8},{1,9},{2,10},{3,11},{4,12},{5,13},{6,14},{7,15},{8,0},{9,1},... | collective-permute-start | bytes 442376 | tf_op jit(solution)/shard_map/ppermute | solution.py:241
  29.2 6.4 %collective-permute-start.9 = (f32[2,128,256]{2,1,0:T(8,128)S(1)}, f32[2,128,256]{2,1,0:T(8,128)S(1)}, u32[]{:S(2)}, u32[]{:S(2)}) collective-permute-start(f32[2,128,256]{2,1,0:T(8,128)S(1)} %get-tuple-element.32), channel_id=1, source_target_pairs={{0,1},{1,0},{2,3},{3,2},{4,5},{5,4},{6,7},{7,6},{8,9},{9,8},{10,11... | collective-permute-start | bytes 786440 | tf_op jit(solution)/shard_map/ppermute | solution.py:232
  35.5 3.5 %collective-permute-start.10 = (f32[16,72,128]{2,1,0:T(8,128)S(1)}, f32[16,72,128]{2,1,0:T(8,128)S(1)}, u32[]{:S(2)}, u32[]{:S(2)}) collective-permute-start(f32[16,72,128]{2,1,0:T(8,128)S(1)} %pad_maximum_fusion.held), channel_id=1, source_target_pairs={{0,2},{1,3},{2,0},{3,1},{4,6},{5,7},{6,4},{7,5},{8,10},{9,11},{10,... | collective-permute-start | bytes 1769480 | tf_op jit(solution)/shard_map/ppermute | solution.py:326
  35.6 5.3 %collective-permute-start.11 = (f32[128,256]{1,0:T(8,128)S(1)}, f32[128,256]{1,0:T(8,128)S(1)}, u32[]{:S(2)}, u32[]{:S(2)}) collective-permute-start(f32[128,256]{1,0:T(8,128)S(1)} %get-tuple-element.40), channel_id=1, source_target_pairs={{0,30},{1,31},{2,0},{3,1},{4,2},{5,3},{6,4},{7,5},{8,6},{9,7},{10,... | collective-permute-start | bytes 393224 | tf_op jit(solution)/shard_map/ppermute | solution.py:232

commit v6 on v5

--- a/solution.py
+++ b/solution.py
@@ -321,7 +321,7 @@
     held, pairs = lax.optimization_barrier((held, pairs))
     arrived = [permute(pairs[k], shards, reps, 0, k) for k in range(1, reps)]
     for i in range(2, len(order), 2):
-        held = exchange(held, order[i : i + 2], index, total)
+        held = exchange(held, order[i : i + 2][::-1], index, total)
     held, arrived = lax.optimization_barrier((held, arrived))
     theirs = lax.ppermute(held, AXES, [(d, d ^ (1 << low)) for d in range(total)])
     summed = pairs[0]

time: 41.7 us -> 41.7 us (level)
  transfers between devices with their start and end apart: 12 -> 12, of which waited for: 6 -> 7; matrix products, arithmetic and copies ran while one was open for 5% -> 5% of each run, Pallas kernels for 17% -> 17%
where the time goes in v6:
time: 41.7 us; the launch traced here: 41.5 us
  starting transfers between devices  16.5 us (40%)
  Pallas kernels  12.4 us (30%)
  waiting for transfers between devices  8.42 us (20%)
  other arithmetic  2.64 us (6%)
  between operations  1.48 us (4%)
    ppermute x5, starting transfers between devices, permute(): return lax.ppermute(value, AXES, route)  8.5 us
    ppermute x6, starting transfers between devices, exchange(): lax.ppermute(held, AXES, [(d, d ^ flip) for d in range(total)])  8.01 us
    pallas_call x1, Pallas kernels, local(): pl.pallas_call(functools.partial(tiles_kernel, reps), out_shape=[jax.Shap...  5.5 us
    ppermute x6, waiting for transfers between devices, exchange(): lax.ppermute(held, AXES, [(d, d ^ flip) for d in range(total)])  4.76 us
    ppermute x5, waiting for transfers between devices, permute(): return lax.ppermute(value, AXES, route)  3.66 us
    pallas_call x1, Pallas kernels, local(): pl.pallas_call(tails_kernel, out_shape=[jax.ShapeDtypeStruct((2, block, w...  2.49 us
    pallas_call x1, Pallas kernels, local(): pl.pallas_call(prepare_kernel, out_shape=(jax.ShapeDtypeStruct((tiles, pa...  2.24 us
    pallas_call x2, Pallas kernels, combine(): pl.pallas_call(kernel, out_shape=jax.ShapeDtypeStruct((rels, width), F32)...  2.23 us
  transfers between devices with their start and end apart: 12, of which 7 were waited for; matrix products, arithmetic and copies ran while one was open for 5% of the time, Pallas kernels for 17%

profile of v6, /device:TPU:0, one launch (start us, length us, event | category | flops | bytes accessed | tf_op | source)
XLA Modules:
  0.0 41.5 jit_solution(10744162661228580635)
XLA Ops:
  0.6 2.4 %collective-permute-start = (f32[128,256]{1,0:T(8,128)}, f32[128,256]{1,0:T(8,128)S(1)}, u32[]{:S(2)}, u32[]{:S(2)}) collective-permute-start(f32[128,256]{1,0:T(8,128)} %entity.1), channel_id=1, source_target_pairs={{0,3},{1,2},{2,5},{3,4},{4,7},{5,6},{6,9},{7,8},{8,11},{9,10},{10,... | collective-permute-start | bytes 393224 | tf_op jit(solution)/shard_map/ppermute | solution.py:232
  3.1 1.6 %collective-permute-start.1 = (f32[128,256]{1,0:T(8,128)}, f32[128,256]{1,0:T(8,128)S(1)}, u32[]{:S(2)}, u32[]{:S(2)}) collective-permute-start(f32[128,256]{1,0:T(8,128)} %entity.1), channel_id=1, source_target_pairs={{0,2},{1,3},{2,4},{3,5},{4,6},{5,7},{6,8},{7,9},{8,10},{9,11},{10,... | collective-permute-start | bytes 393224 | tf_op jit(solution)/shard_map/ppermute | solution.py:232
  4.7 0.5 %collective-permute-start.2 = (f32[128,256]{1,0:T(8,128)}, f32[128,256]{1,0:T(8,128)}, u32[]{:S(2)}, u32[]{:S(2)}) collective-permute-start(f32[128,256]{1,0:T(8,128)} %entity.1), channel_id=1, source_target_pairs={{0,1},{1,0},{2,3},{3,2},{4,5},{5,4},{6,7},{7,6},{8,9},{9,8},{10,11... | collective-permute-start | bytes 393224 | tf_op jit(solution)/shard_map/ppermute | solution.py:232
  5.9 1.8 %convert_element_type.3.refs_8_ = f32[32,128,128]{2,1,0:T(8,128)S(1)} convert(s32[32,128,128]{2,1,0:T(8,128)} %param.13) | non-fusion elementwise | flops 524288 | bytes 4194304 | tf_op jit(solution)/shard_map/convert_element_type | solution.py:279
  7.8 2.2 %prepare.1 = (f32[32,256]{1,0:T(8,128)S(1)}, f32[32,256]{1,0:T(8,128)S(1)}, f32[1,128]{1,0:T(1,128)S(1)}, f32[128,256]{1,0:T(8,128)S(1)}) custom-call(s32[1]{0:T(128)S(6)} %copy.10.count.refs_0_, s32[32]{0:T(128)S(1)} %copy-done.3, s32[32,256]{1,0:T(8,128)S(1)} %copy-done.2, f32[900,256]{1,0:T(8,128)S(1)} %copy-done, f32[128,256]{1,0:T(8,128)S(1)} %copy-done.1), custom_call_target="tpu_custom_call" | custom-call | flops 4194304 | bytes 4194304 | tf_op jit(solution)/shard_map/prepare/pallas_call | solution.py:259
  10.1 1.8 %collective-permute-done.1.refs_5_ = f32[128,256]{1,0:T(8,128)S(1)} collective-permute-done((f32[128,256]{1,0:T(8,128)}, f32[128,256]{1,0:T(8,128)S(1)}, u32[]{:S(2)}, u32[]{:S(2)}) %collective-permute-start.1) | collective-permute-done | bytes 131104 | tf_op jit(solution)/shard_map/ppermute | solution.py:232
  11.8 5.5 %tiles.1 = (f32[72,128]{1,0:T(8,128)S(1)}, f32[2,128,256]{2,1,0:T(8,128)S(1)}, f32[2,128,256]{2,1,0:T(8,128)S(1)}, bf16[4096,256]{1,0:T(8,128)(2,1)S(1)}, bf16[4096,256]{1,0:T(8,128)(2,1)S(1)}) custom-call(s32[1]{0:T(128)S(6)} %copy.10.count.refs_0_, s32[1]{0:T(128)} %bitcast.refs_1_.place, s32[32]{0:T(128)S(1)} %copy-done.5, s32[32]{0:T(128)S(1)} %copy-done.4, ...), custom_call_target="tpu_custom_call" | custom-call | flops 3221225472 | bytes 4194304 | tf_op jit(solution)/shard_map/tiles/pallas_call | solution.py:283
  17.3 2.2 %collective-permute-start.3 = (f32[1,72,128]{2,1,0:T(8,128)S(1)}, f32[1,72,128]{2,1,0:T(8,128)S(1)}, u32[]{:S(2)}, u32[]{:S(2)}) collective-permute-start(f32[1,72,128]{2,1,0:T(8,128)S(1)} %bitcast.10), channel_id=1, source_target_pairs={{0,17},{1,16},{2,19},{3,18},{4,21},{5,20},{6,23},{7,22},{8,25},{9,... | collective-permute-start | bytes 110600 | tf_op jit(solution)/shard_map/ppermute | solution.py:241
  19.5 1.2 %collective-permute-start.4 = (f32[1,72,128]{2,1,0:T(8,128)S(1)}, f32[1,72,128]{2,1,0:T(8,128)S(1)}, u32[]{:S(2)}, u32[]{:S(2)}) collective-permute-start(f32[1,72,128]{2,1,0:T(8,128)S(1)} %bitcast.11), channel_id=1, source_target_pairs={{0,1},{1,0},{2,3},{3,2},{4,5},{5,4},{6,7},{7,6},{8,9},{9,8},{10,11... | collective-permute-start | bytes 110600 | tf_op jit(solution)/shard_map/ppermute | solution.py:241
  20.7 1.1 %collective-permute-start.5 = (f32[1,72,128]{2,1,0:T(8,128)S(1)}, f32[1,72,128]{2,1,0:T(8,128)S(1)}, u32[]{:S(2)}, u32[]{:S(2)}) collective-permute-start(f32[1,72,128]{2,1,0:T(8,128)S(1)} %bitcast.12), channel_id=1, source_target_pairs={{0,16},{1,17},{2,18},{3,19},{4,20},{5,21},{6,22},{7,23},{8,24},{9,... | collective-permute-start | bytes 110600 | tf_op jit(solution)/shard_map/ppermute | solution.py:241
  21.8 2.5 %tails.1 = (f32[2,128,256]{2,1,0:T(8,128)S(1)}, f32[2,128,256]{2,1,0:T(8,128)S(1)}) custom-call(s32[1]{0:T(128)} %bitcast.refs_1_.place, s32[32]{0:T(128)S(1)} %copy-done.5, f32[2,128,256]{2,1,0:T(8,128)S(1)} %get-tuple-element.24.head_parts, f32[2,128,256]{2,1,0:T(8,128)S(1)} %get-tuple-element.25.heads, f32[32,256]{1,0:T(8,128)S(1)} %get-tuple-element.21.refs_10_.weights, ...), custom_call_target="tpu_custom_call" | custom-call | flops 1610612736 | bytes 4194304 | tf_op jit(solution)/shard_map/tails/pallas_call | solution.py:298
  24.3 1.3 %collective-permute-done.5 = f32[1,72,128]{2,1,0:T(8,128)S(1)} collective-permute-done((f32[1,72,128]{2,1,0:T(8,128)S(1)}, f32[1,72,128]{2,1,0:T(8,128)S(1)}, u32[]{:S(2)}, u32[]{:S(2)}) %collective-permute-start.5) | collective-permute-done | bytes 36896 | tf_op jit(solution)/shard_map/ppermute | solution.py:241
  25.6 2.6 %collective-permute-start.6 = (f32[4,72,128]{2,1,0:T(8,128)S(1)}, f32[4,72,128]{2,1,0:T(8,128)S(1)}, u32[]{:S(2)}, u32[]{:S(2)}) collective-permute-start(f32[4,72,128]{2,1,0:T(8,128)S(1)} %pad_maximum_fusion.1), channel_id=1, source_target_pairs={{0,12},{1,13},{2,14},{3,15},{4,8},{5,9},{6,10},{7,11},{8,4},{9,5},... | collective-permute-start | bytes 442376 | tf_op jit(solution)/shard_map/ppermute | solution.py:241
  28.2 0.5 %collective-permute-start.7 = (f32[4,72,128]{2,1,0:T(8,128)S(1)}, f32[4,72,128]{2,1,0:T(8,128)S(1)}, u32[]{:S(2)}, u32[]{:S(2)}) collective-permute-start(f32[4,72,128]{2,1,0:T(8,128)S(1)} %pad_maximum_fusion.1), channel_id=1, source_target_pairs={{0,8},{1,9},{2,10},{3,11},{4,12},{5,13},{6,14},{7,15},{8,0},{9,1},... | collective-permute-start | bytes 442376 | tf_op jit(solution)/shard_map/ppermute | solution.py:241
  28.7 0.5 %collective-permute-start.8 = (f32[4,72,128]{2,1,0:T(8,128)S(1)}, f32[4,72,128]{2,1,0:T(8,128)S(1)}, u32[]{:S(2)}, u32[]{:S(2)}) collective-permute-start(f32[4,72,128]{2,1,0:T(8,128)S(1)} %pad_maximum_fusion.1), channel_id=1, source_target_pairs={{0,4},{1,5},{2,6},{3,7},{4,0},{5,1},{6,2},{7,3},{8,12},{9,13},{10,... | collective-permute-start | bytes 442376 | tf_op jit(solution)/shard_map/ppermute | solution.py:241
  29.2 1.2 %collective-permute-start.9 = (f32[2,128,256]{2,1,0:T(8,128)S(1)}, f32[2,128,256]{2,1,0:T(8,128)S(1)}, u32[]{:S(2)}, u32[]{:S(2)}) collective-permute-start(f32[2,128,256]{2,1,0:T(8,128)S(1)} %get-tuple-element.32), channel_id=1, source_target_pairs={{0,1},{1,0},{2,3},{3,2},{4,5},{5,4},{6,7},{7,6},{8,9},{9,8},{10,11... | collective-permute-start | bytes 786440 | tf_op jit(solution)/shard_map/ppermute | solution.py:232
  30.3 1.7 %collective-permute-done.6 = f32[4,72,128]{2,1,0:T(8,128)S(1)} collective-permute-done((f32[4,72,128]{2,1,0:T(8,128)S(1)}, f32[4,72,128]{2,1,0:T(8,128)S(1)}, u32[]{:S(2)}, u32[]{:S(2)}) %collective-permute-start.6) | collective-permute-done | bytes 147488 | tf_op jit(solution)/shard_map/ppermute | solution.py:241
  32.0 1.6 %collective-permute-done.7 = f32[4,72,128]{2,1,0:T(8,128)S(1)} collective-permute-done((f32[4,72,128]{2,1,0:T(8,128)S(1)}, f32[4,72,128]{2,1,0:T(8,128)S(1)}, u32[]{:S(2)}, u32[]{:S(2)}) %collective-permute-start.7) | collective-permute-done | bytes 147488 | tf_op jit(solution)/shard_map/ppermute | solution.py:241
  33.9 1.6 %collective-permute-done.9 = f32[2,128,256]{2,1,0:T(8,128)S(1)} collective-permute-done((f32[2,128,256]{2,1,0:T(8,128)S(1)}, f32[2,128,256]{2,1,0:T(8,128)S(1)}, u32[]{:S(2)}, u32[]{:S(2)}) %collective-permute-start.9) | collective-permute-done | bytes 262176 | tf_op jit(solution)/shard_map/ppermute | solution.py:232
  35.6 2.7 %collective-permute-start.11 = (f32[128,256]{1,0:T(8,128)S(1)}, f32[128,256]{1,0:T(8,128)S(1)}, u32[]{:S(2)}, u32[]{:S(2)}) collective-permute-start(f32[128,256]{1,0:T(8,128)S(1)} %get-tuple-element.40), channel_id=1, source_target_pairs={{0,30},{1,31},{2,0},{3,1},{4,2},{5,3},{6,4},{7,5},{8,6},{9,7},{10,... | collective-permute-start | bytes 393224 | tf_op jit(solution)/shard_map/ppermute | solution.py:232
  38.4 0.6 %combine.2.before = f32[900,256]{1,0:T(8,128)S(1)} custom-call(f32[16,72,128]{2,1,0:T(8,128)S(1)} %pad_maximum_fusion.held), custom_call_target="tpu_custom_call" | custom-call | flops 471859200 | bytes 2097152 | tf_op jit(solution)/shard_map/combine/pallas_call | solution.py:210
  39.0 1.6 %combine.3 = f32[900,256]{1,0:T(8,128)} custom-call(f32[16,72,128]{2,1,0:T(8,128)S(1)} %collective-permute-done.10.gathered, f32[900,256]{1,0:T(8,128)S(1)} %combine.2.before), custom_call_target="tpu_custom_call" | custom-call | flops 471859200 | bytes 2097152 | tf_op jit(solution)/shard_map/combine/pallas_call | solution.py:210
  40.6 0.3 collective-permute-done.11
  40.9 0.7 %add.19 = f32[128,256]{1,0:T(8,128)} add(f32[128,256]{1,0:T(8,128)S(1)} %get-tuple-element.35, f32[128,256]{1,0:T(8,128)S(1)} %collective-permute-done.11) | non-fusion elementwise | flops 32768 | bytes 393216 | tf_op jit(solution)/shard_map/add | solution.py:334
  (25 shorter events, 0.4 us)
Async XLA Ops:
  0.6 9.4 %collective-permute-start = (f32[128,256]{1,0:T(8,128)}, f32[128,256]{1,0:T(8,128)S(1)}, u32[]{:S(2)}, u32[]{:S(2)}) collective-permute-start(f32[128,256]{1,0:T(8,128)} %entity.1), channel_id=1, source_target_pairs={{0,3},{1,2},{2,5},{3,4},{4,7},{5,6},{6,9},{7,8},{8,11},{9,10},{10,... | collective-permute-start | bytes 393224 | tf_op jit(solution)/shard_map/ppermute | solution.py:232
  3.1 8.7 %collective-permute-start.1 = (f32[128,256]{1,0:T(8,128)}, f32[128,256]{1,0:T(8,128)S(1)}, u32[]{:S(2)}, u32[]{:S(2)}) collective-permute-start(f32[128,256]{1,0:T(8,128)} %entity.1), channel_id=1, source_target_pairs={{0,2},{1,3},{2,4},{3,5},{4,6},{5,7},{6,8},{7,9},{8,10},{9,11},{10,... | collective-permute-start | bytes 393224 | tf_op jit(solution)/shard_map/ppermute | solution.py:232
  4.7 7.1 %collective-permute-start.2 = (f32[128,256]{1,0:T(8,128)}, f32[128,256]{1,0:T(8,128)}, u32[]{:S(2)}, u32[]{:S(2)}) collective-permute-start(f32[128,256]{1,0:T(8,128)} %entity.1), channel_id=1, source_target_pairs={{0,1},{1,0},{2,3},{3,2},{4,5},{5,4},{6,7},{7,6},{8,9},{9,8},{10,11... | collective-permute-start | bytes 393224 | tf_op jit(solution)/shard_map/ppermute | solution.py:232
  5.9 1.9 %copy-start = (f32[900,256]{1,0:T(8,128)S(1)}, f32[900,256]{1,0:T(8,128)}, u32[]{:S(2)}) copy-start(f32[900,256]{1,0:T(8,128)} %rel_weight.1) | copy-start | bytes 2764804
  5.9 1.9 %copy-start.1 = (f32[128,256]{1,0:T(8,128)S(1)}, f32[128,256]{1,0:T(8,128)}, u32[]{:S(2)}) copy-start(f32[128,256]{1,0:T(8,128)} %entity.1) | copy-start | bytes 393220
  5.9 1.9 %copy-start.2 = (s32[32,256]{1,0:T(8,128)S(1)}, s32[32,256]{1,0:T(8,128)}, u32[]{:S(2)}) copy-start(s32[32,256]{1,0:T(8,128)} %negatives.1) | copy-start | bytes 98308
  5.9 1.9 %copy-start.3 = (s32[32]{0:T(128)S(1)}, s32[32]{0:T(128)}, u32[]{:S(2)}) copy-start(s32[32]{0:T(128)} %rel_ids.1) | copy-start | bytes 388
  5.9 5.9 %copy-start.4 = (s32[32]{0:T(128)S(1)}, s32[32]{0:T(128)}, u32[]{:S(2)}) copy-start(s32[32]{0:T(128)} %refs_3_.1) | copy-start | bytes 388
  5.9 5.9 %copy-start.5 = (s32[32]{0:T(128)S(1)}, s32[32]{0:T(128)}, u32[]{:S(2)}) copy-start(s32[32]{0:T(128)} %head_in_ids.1) | copy-start | bytes 388
  17.3 7.0 %collective-permute-start.3 = (f32[1,72,128]{2,1,0:T(8,128)S(1)}, f32[1,72,128]{2,1,0:T(8,128)S(1)}, u32[]{:S(2)}, u32[]{:S(2)}) collective-permute-start(f32[1,72,128]{2,1,0:T(8,128)S(1)} %bitcast.10), channel_id=1, source_target_pairs={{0,17},{1,16},{2,19},{3,18},{4,21},{5,20},{6,23},{7,22},{8,25},{9,... | collective-permute-start | bytes 110600 | tf_op jit(solution)/shard_map/ppermute | solution.py:241
  19.5 4.8 %collective-permute-start.4 = (f32[1,72,128]{2,1,0:T(8,128)S(1)}, f32[1,72,128]{2,1,0:T(8,128)S(1)}, u32[]{:S(2)}, u32[]{:S(2)}) collective-permute-start(f32[1,72,128]{2,1,0:T(8,128)S(1)} %bitcast.11), channel_id=1, source_target_pairs={{0,1},{1,0},{2,3},{3,2},{4,5},{5,4},{6,7},{7,6},{8,9},{9,8},{10,11... | collective-permute-start | bytes 110600 | tf_op jit(solution)/shard_map/ppermute | solution.py:241
  20.7 4.9 %collective-permute-start.5 = (f32[1,72,128]{2,1,0:T(8,128)S(1)}, f32[1,72,128]{2,1,0:T(8,128)S(1)}, u32[]{:S(2)}, u32[]{:S(2)}) collective-permute-start(f32[1,72,128]{2,1,0:T(8,128)S(1)} %bitcast.12), channel_id=1, source_target_pairs={{0,16},{1,17},{2,18},{3,19},{4,20},{5,21},{6,22},{7,23},{8,24},{9,... | collective-permute-start | bytes 110600 | tf_op jit(solution)/shard_map/ppermute | solution.py:241
  25.6 6.4 %collective-permute-start.6 = (f32[4,72,128]{2,1,0:T(8,128)S(1)}, f32[4,72,128]{2,1,0:T(8,128)S(1)}, u32[]{:S(2)}, u32[]{:S(2)}) collective-permute-start(f32[4,72,128]{2,1,0:T(8,128)S(1)} %pad_maximum_fusion.1), channel_id=1, source_target_pairs={{0,12},{1,13},{2,14},{3,15},{4,8},{5,9},{6,10},{7,11},{8,4},{9,5},... | collective-permute-start | bytes 442376 | tf_op jit(solution)/shard_map/ppermute | solution.py:241
  28.2 5.4 %collective-permute-start.7 = (f32[4,72,128]{2,1,0:T(8,128)S(1)}, f32[4,72,128]{2,1,0:T(8,128)S(1)}, u32[]{:S(2)}, u32[]{:S(2)}) collective-permute-start(f32[4,72,128]{2,1,0:T(8,128)S(1)} %pad_maximum_fusion.1), channel_id=1, source_target_pairs={{0,8},{1,9},{2,10},{3,11},{4,12},{5,13},{6,14},{7,15},{8,0},{9,1},... | collective-permute-start | bytes 442376 | tf_op jit(solution)/shard_map/ppermute | solution.py:241
  28.7 5.1 %collective-permute-start.8 = (f32[4,72,128]{2,1,0:T(8,128)S(1)}, f32[4,72,128]{2,1,0:T(8,128)S(1)}, u32[]{:S(2)}, u32[]{:S(2)}) collective-permute-start(f32[4,72,128]{2,1,0:T(8,128)S(1)} %pad_maximum_fusion.1), channel_id=1, source_target_pairs={{0,4},{1,5},{2,6},{3,7},{4,0},{5,1},{6,2},{7,3},{8,12},{9,13},{10,... | collective-permute-start | bytes 442376 | tf_op jit(solution)/shard_map/ppermute | solution.py:241
  29.2 6.4 %collective-permute-start.9 = (f32[2,128,256]{2,1,0:T(8,128)S(1)}, f32[2,128,256]{2,1,0:T(8,128)S(1)}, u32[]{:S(2)}, u32[]{:S(2)}) collective-permute-start(f32[2,128,256]{2,1,0:T(8,128)S(1)} %get-tuple-element.32), channel_id=1, source_target_pairs={{0,1},{1,0},{2,3},{3,2},{4,5},{5,4},{6,7},{7,6},{8,9},{9,8},{10,11... | collective-permute-start | bytes 786440 | tf_op jit(solution)/shard_map/ppermute | solution.py:232
  35.5 3.5 %collective-permute-start.10 = (f32[16,72,128]{2,1,0:T(8,128)S(1)}, f32[16,72,128]{2,1,0:T(8,128)S(1)}, u32[]{:S(2)}, u32[]{:S(2)}) collective-permute-start(f32[16,72,128]{2,1,0:T(8,128)S(1)} %pad_maximum_fusion.held), channel_id=1, source_target_pairs={{0,2},{1,3},{2,0},{3,1},{4,6},{5,7},{6,4},{7,5},{8,10},{9,11},{10,... | collective-permute-start | bytes 1769480 | tf_op jit(solution)/shard_map/ppermute | solution.py:326
  35.6 5.3 %collective-permute-start.11 = (f32[128,256]{1,0:T(8,128)S(1)}, f32[128,256]{1,0:T(8,128)S(1)}, u32[]{:S(2)}, u32[]{:S(2)}) collective-permute-start(f32[128,256]{1,0:T(8,128)S(1)} %get-tuple-element.40), channel_id=1, source_target_pairs={{0,30},{1,31},{2,0},{3,1},{4,2},{5,3},{6,4},{7,5},{8,6},{9,7},{10,... | collective-permute-start | bytes 393224 | tf_op jit(solution)/shard_map/ppermute | solution.py:232
